TPU v7x, 256 devices: a whole 4x4x8 slice. The times are simulated.
256 devices in a mesh: lat: 16 (over z, core), lon: 16 (over y, x).
Axes of the slice: x: 4, y: 4, z: 8, core: 2. Of those that a mesh axis runs over, the one named last changes fastest.
Arguments:
- increments: float32 [2, 8, 512, 6144], P(None, None, 'lat', 'lon'), may hold values from -4 to 4
- ens_winds: bfloat16 [2, 8, 128, 1536], P(None, None, 'lat', 'lon'), may hold values from -6 to 6
- lat_offsets: int32 [16], P('lat'), may hold values from 4 to 116, as said below
- lon_offsets: int32 [16], P('lon'), may hold values from -4 to 1444, as said below
Outputs:
- potentials: float32 [2, 8, 512, 6144], P(None, None, 'lat', 'lon')
Inputs may be any that keep to these rules, and one draw needn't show every extreme that they name: `lat_offsets`: the offset of tile row i is i * 8 plus a jitter of at most 4 in size; the first tile row's jitter is exactly +4, the last one's exactly -4. `lon_offsets`: the offset of tile column j is j * 96 plus a jitter of at most 4 in size; the first tile column's jitter is exactly -4, the last one's exactly +4; columns are read modulo 1536.
All inputs are finite; a program needn't handle non-finite values.
Results may differ from a plain program's by a relative error of at most 0.0009.
Values may be sent and summed in bfloat16 or wider, within the bound.
No kernel may reach another device: no remote copies, remote signals or barrier semaphores. Data moves between devices by JAX's collectives and lax.ppermute only.
A program may use at most 128 MiB of HBM per device.

v0:
```python
import functools

import jax
import jax.numpy as jnp
import ml_dtypes
import numpy as np
from jax import lax
from jax.experimental import pallas as pl
from jax.experimental.pallas import tpu as pltpu
from jax.sharding import PartitionSpec as P

CLAT = 32
GRIDS = 5
OMEGA = 0.8
CYCLES = 2
ROWS = 64
PHASES = 8
LEAD = 40
INC_SCALE = 2.0**13
WIND_SCALE = 2.0**12
OUT_EXP = 14.0
OWN_ROWS = 112
HALO_ROWS = 80

f32 = jnp.float32
bf16 = jnp.bfloat16


def column_of(n):
    return 8 * (n % 128 - LEAD) + n // 128


def spread_table():
    columns = column_of(np.arange(1024))
    return (np.arange(896)[:, None] - 256 == columns[None, :]).astype(ml_dtypes.bfloat16)


def collect_table():
    columns = column_of(np.arange(1024))
    return (columns[:, None] == np.arange(384)[None, :]).astype(ml_dtypes.bfloat16)


def centre(level):
    return 4.0 + 4.0**level * 0.25 / (CLAT * CLAT)


def west(v, hop):
    first = pltpu.roll(v[-1], hop, 1)[None]
    return jnp.concatenate([first, v[:-1]], 0) if v.shape[0] > 1 else first


def east(v, hop):
    last = pltpu.roll(v[0], 128 - hop, 1)[None]
    return jnp.concatenate([v[1:], last], 0) if v.shape[0] > 1 else last


def above_first(v):
    lanes = lax.broadcasted_iota(jnp.int32, (8, 128), 0)
    return jnp.stack([jnp.where(lanes > 0, pltpu.roll(v[p], 1, 0), 0.0) for p in range(v.shape[0])])


def below_last(v):
    lanes = lax.broadcasted_iota(jnp.int32, (8, 128), 0)
    return jnp.stack([jnp.where(lanes < 7, pltpu.roll(v[p], 7, 0), 0.0) for p in range(v.shape[0])])


def doubled(v, phases):
    if v.shape[0] == phases:
        return v
    return jnp.concatenate([v[p // 2][None] for p in range(phases)], 0)


def loop(count, body, carry, unroll):
    if unroll >= count:
        for step in range(count):
            carry = body(step, carry)
        return carry
    return lax.fori_loop(0, count, body, carry, unroll=unroll)


def shape_of(level):
    return ROWS >> level, max(PHASES >> level, 1), (2 if level == GRIDS - 1 else 1)


UNROLL = (2, 4, 8, 4, 2)


def sweep(level, x, b, start=None, coarse=None):
    rows, phases, hop = shape_of(level)
    gain = OMEGA / centre(level)
    if start is not None:
        old = lambda r, s: b[r] * gain
    elif coarse is not None:
        old = lambda r, s: x[r] + doubled(coarse[s], phases)
    else:
        old = lambda r, s: x[r]
    first = old(0, 0)
    top = above_first(old(rows - 1, rows // 2 - 1))
    if start is None:
        x[rows] = below_last(first)

    def body(s, carry):
        prev, c0 = carry
        c1 = old(2 * s + 1, s)
        n = old(2 * s + 2, s + 1)
        x[2 * s] = 0.2 * c0 + gain * ((b[2 * s] + prev) + c1 + (west(c0, hop) + east(c0, hop)))
        x[2 * s + 1] = 0.2 * c1 + gain * ((b[2 * s + 1] + c0) + n + (west(c1, hop) + east(c1, hop)))
        return c1, n

    loop(rows // 2, body, (top, first), UNROLL[level])


def residual(level, x, b, out):
    rows, phases, hop = shape_of(level)
    weight = centre(level)
    first = x[0]
    top = above_first(x[rows - 1])
    x[rows] = below_last(first)

    def body(s, carry):
        prev, c0 = carry
        c1 = x[2 * s + 1]
        n = x[2 * s + 2]
        r0 = (b[2 * s] + prev) + (c1 + (west(c0, hop) + east(c0, hop))) - weight * c0
        r1 = (b[2 * s + 1] + c0) + (n + (west(c1, hop) + east(c1, hop))) - weight * c1
        t = r0 + r1
        if phases > 1:
            out[s] = jnp.concatenate([(t[2 * p] + t[2 * p + 1])[None] for p in range(phases // 2)], 0)
        else:
            lane = lax.broadcasted_iota(jnp.int32, (8, 128), 1)
            out[s] = t + jnp.where(lane % 2 == 0, pltpu.roll(t[0], 127, 1), pltpu.roll(t[0], 1, 1))[None]
        return c1, n

    loop(rows // 2, body, (top, first), UNROLL[level])
    out[rows // 2] = below_last(out[0])


def vcycle(level, x, b, fresh):
    rows = shape_of(level)[0]
    if level == GRIDS - 1:
        sweep(level, x[level], b[level], start=True)
        sweep(level, x[level], b[level])
    else:
        if fresh:
            sweep(level, x[level], b[level], start=True)
        else:
            sweep(level, x[level], b[level])
            sweep(level, x[level], b[level])
        residual(level, x[level], b[level], b[level + 1])
        vcycle(level + 1, x, b, True)
        sweep(level, x[level], b[level], coarse=x[level + 1])
    sweep(level, x[level], b[level])
    if level > 0:
        x[level][rows] = jnp.zeros(x[level].shape[1:], f32)


def hat(position, index):
    return jnp.maximum(1.0 - jnp.abs(position - index), 0.0)


def kernel(own, left, right, spread, collect, out, x0, x1, x2, x3, x4, b0, b1, b2, b3, b4, inc, gx, gy, split):
    x = (x0, x1, x2, x3, x4)
    b = (b0, b1, b2, b3, b4)
    pieces = ((left, 0, HALO_ROWS), (left, 48, HALO_ROWS), (own, 0, OWN_ROWS), (own, 32, OWN_ROWS), (own, 80, OWN_ROWS), (right, 0, HALO_ROWS), (right, 32, HALO_ROWS))
    for j, (ref, at, height) in enumerate(pieces):
        block = jnp.concatenate([ref[i * height + at : i * height + at + 32, :] for i in range(16)], 0) * (1.0 / INC_SCALE)
        high = block.astype(bf16)
        split[0:512, 128 * j : 128 * j + 128] = high
        split[512:1024, 128 * j : 128 * j + 128] = (block - high.astype(f32)).astype(bf16)
    for p in range(PHASES):
        table = spread[:, 128 * p : 128 * p + 128]
        inc[512 * p : 512 * p + 512, :] = jnp.dot(split[0:512, 0:896], table, preferred_element_type=f32) + jnp.dot(
            split[512:1024, 0:896], table, preferred_element_type=f32
        )
    lane = lax.broadcasted_iota(jnp.int32, (8, 128), 1).astype(f32)
    parts = []
    for half in range(2):
        first = own[pl.ds(OWN_ROWS * half + 64, 8, stride=2 * OWN_ROWS), :][:, 96:97]
        for a in range(32):
            parts.append(hat(first + a * 0.25, lane))
    row_table = jnp.concatenate(parts, 0).astype(bf16)

    def winds(offset):
        cols = []
        for ref, at, height in ((left, 32, HALO_ROWS), (own, 64, OWN_ROWS), (right, 64, HALO_ROWS)):
            rows = [ref[i * height + at + offset : i * height + at + offset + 8, :] for i in range(16)]
            cols.append(jnp.concatenate(rows, 0) * (1.0 / WIND_SCALE))
        table = jnp.concatenate(cols, 1).astype(bf16)
        return jnp.dot(row_table, table, preferred_element_type=f32).astype(bf16)

    wx = winds(0)
    wy = winds(8)
    n = lax.broadcasted_iota(jnp.int32, (1, 1024), 1)
    column = 8 * ((n & 127) - LEAD) + (n >> 7)
    shift_left = left[32:33, 97:98]
    shift_own = own[64:65, 97:98]
    shift_right = right[64:65, 97:98]

    def place(c):
        value = c.astype(f32) * 0.25
        return value + 96.0 + jnp.where(c < 0, shift_left, jnp.where(c < 384, shift_own, shift_right))

    m = lax.broadcasted_iota(jnp.int32, (384, 1), 0)
    index = jnp.where((m & 127) < 96, (m >> 7) * 96 + (m & 127), -1000).astype(f32)
    here = place(column)
    gx[...] = jnp.dot(
        wx, (2.0 * (hat(place(column + 1), index) - hat(place(column - 1), index))).astype(bf16), preferred_element_type=f32
    )
    gy[...] = jnp.dot(wy, (2.0 * hat(here, index)).astype(bf16), preferred_element_type=f32)

    def cut(ref, r):
        rows = pl.ds(pl.multiple_of(8 * r, 8), 8)
        return jnp.stack([ref[rows, 128 * p : 128 * p + 128] for p in range(PHASES)])

    def force(r, above, below):
        mine = jnp.stack([inc[pl.ds(512 * p + r, 8, stride=64), :] for p in range(PHASES)])
        b0[r] = mine + cut(gx, r) + (below - above)

    first = cut(gy, 0)
    final = cut(gy, ROWS - 1)

    def force_row(r, carry):
        above, here = carry
        below = cut(gy, r + 1)
        force(r, above, below)
        return here, below

    above, _ = lax.fori_loop(0, ROWS - 1, force_row, (above_first(final), first))
    force(ROWS - 1, above, below_last(first))
    b0[ROWS] = below_last(b0[0])

    for cycle in range(CYCLES):
        vcycle(0, x, b, cycle == 0)

    def peak(r, carry):
        return jnp.maximum(carry, jnp.max(jnp.abs(x0[r]), axis=0))

    top = lax.fori_loop(0, ROWS, peak, jnp.zeros((8, 128), f32))
    lane = lax.broadcasted_iota(jnp.int32, (8, 128), 1)
    top = jnp.max(jnp.where((lane >= LEAD) & (lane < LEAD + 48), top, 0.0), axis=(0, 1), keepdims=True)
    power = jnp.ceil(jnp.log2(jnp.maximum(top, 1e-30)))
    scale = jnp.exp2(OUT_EXP - power)

    def pack(s, carry):
        pair = jnp.concatenate([x0[2 * s], x0[2 * s + 1]], 1) * scale
        high = pair.astype(bf16)
        low = (pair - high.astype(f32)).astype(bf16)
        at = pl.multiple_of(16 * s, 16)
        for p in range(PHASES):
            split[pl.ds(at, 16), 128 * p : 128 * p + 128] = high[p]
            split[pl.ds(at + 512, 16), 128 * p : 128 * p + 128] = low[p]
        return carry

    lax.fori_loop(0, ROWS // 2, pack, 0)
    for j in range(3):
        table = collect[:, 128 * j : 128 * j + 128]
        block = jnp.dot(split[0:512, :], table, preferred_element_type=f32) + jnp.dot(
            split[512:1024, :], table, preferred_element_type=f32
        )
        for r in range(ROWS):
            out[pl.ds(OWN_ROWS * (r // 32) + 32 * j + r % 32, 8, stride=2 * OWN_ROWS), :] = block[8 * r : 8 * r + 8, :]
    for i in range(16):
        out[OWN_ROWS * i + 96 : OWN_ROWS * i + 112, :] = jnp.broadcast_to(power, (16, 128))


def core(own, left, right, interpret=False):
    grids = []
    for level in range(GRIDS):
        rows, phases, _ = shape_of(level)
        grids.append(pltpu.VMEM((rows + 1, phases, 8, 128), f32))
    return pl.pallas_call(
        kernel,
        out_shape=jax.ShapeDtypeStruct((16 * OWN_ROWS, 128), f32),
        scratch_shapes=grids
        + grids
        + [
            pltpu.VMEM((512 * PHASES, 128), f32),
            pltpu.VMEM((512, 1024), f32),
            pltpu.VMEM((512, 1024), f32),
            pltpu.VMEM((1024, 1024), bf16),
        ],
        compiler_params=pltpu.CompilerParams(vmem_limit_bytes=48 * 1024 * 1024),
        interpret=interpret,
    )(own, left, right, jnp.asarray(spread_table()), jnp.asarray(collect_table()))


def parcel(increments, ens_winds, lat_first, lon_shift):
    inc = increments.reshape(16, 32, 384) * INC_SCALE
    u, v = ens_winds[0], ens_winds[1]
    across = jnp.concatenate([v, u], 0)
    along = jnp.concatenate([-u, v], 0)
    winds = jnp.concatenate([across, along], 1).astype(f32) * WIND_SCALE
    lane = lax.broadcasted_iota(jnp.int32, (16, 16, 32), 2)
    meta = jnp.where(lane == 0, lat_first, jnp.where(lane == 1, lon_shift, 0)).astype(f32)
    winds = jnp.concatenate([winds, meta], 2)
    return jnp.concatenate([inc[:, :, 0:128], inc[:, :, 128:256], winds, inc[:, :, 256:384]], 1).astype(jnp.float16)


def unpack(got):
    power = got[:, 96:97, 0:1].astype(f32)
    values = got[:, :96].astype(f32) * jnp.exp2(power - OUT_EXP)
    return values.reshape(16, 3, 32, 128).transpose(0, 2, 1, 3).reshape(2, 8, 32, 384)


def local(increments, ens_winds, lat_offsets, lon_offsets):
    count = lax.axis_size("lon")
    me = lax.axis_index("lon")
    mine = parcel(increments, ens_winds, lat_offsets[0], lon_offsets[0] - me * ens_winds.shape[3])
    held = lax.all_to_all(mine, "lat", 0, 0, tiled=True)
    even = me % 2 == 0
    to_right, to_left = held[:, 32:112], held[:, 0:80]
    pairs0 = [(i, i ^ 1) for i in range(count)]
    pairs1 = [(i, (((i - 1) ^ 1) + 1) % count) for i in range(count)]
    got0 = lax.ppermute(jnp.where(even, to_right, to_left), "lon", pairs0)
    got1 = lax.ppermute(jnp.where(even, to_left, to_right), "lon", pairs1)
    left = jnp.where(even, got1, got0).astype(f32).reshape(16 * HALO_ROWS, 128)
    right = jnp.where(even, got0, got1).astype(f32).reshape(16 * HALO_ROWS, 128)
    own = held.astype(f32).reshape(16 * OWN_ROWS, 128)
    done = core(own, left, right).reshape(16, OWN_ROWS, 128).astype(jnp.float16)
    return unpack(lax.all_to_all(done, "lat", 0, 0, tiled=True))


def solution(mesh):
    in_specs = (P(None, None, "lat", "lon"), P(None, None, "lat", "lon"), P("lat"), P("lon"))
    out_specs = P(None, None, "lat", "lon")
    return jax.shard_map(local, mesh=mesh, in_specs=in_specs, out_specs=out_specs, check_vma=False)
```

profile of v0, /device:TPU:1, one launch (start us, length us, event | category | flops | bytes accessed | tf_op | source)
XLA Modules:
  0.0 95.9 jit_solution(454273991029383964)
XLA Ops:
  0.0 0.7 fusion
  0.7 0.7 slice_bitcast_fusion
  2.8 1.2 %multiply_convert_fusion = f16[2,8,32,384]{3,2,1,0:T(8,128)(2,1)S(1)} fusion(f32[2,8,32,384]{3,2,1,0:T(8,128)} %param.6), kind=kLoop, calls=%fused_computation.1 | loop fusion | flops 393216 | bytes 1179648 | tf_op jit(solution)/shard_map/convert.11
  4.0 0.1 fusion.1
  4.1 1.0 %pad_maximum_fusion = f16[16,112,128]{2,1,0:T(8,128)(2,1)} fusion(f16[16,32,128]{2,1,0:T(8,128)(2,1)S(1)} %get-tuple-element.10, f16[16,16,32]{2,1,0:T(8,128)(2,1)S(1)} %convert_convert_fusion, f16[16,16,96]{2,1,0:T(8,128)(2,1)S(1)} %multiply_convert_fusion.1, f16[16,32,128]{2,1,0:T(8,128)(2,1)S(1)} %get-tuple-element.11, ...), kind=kLoop, calls=%fused_computation.2 | loop fusion | flops 917504 | bytes 917504 | tf_op jit(solution)/shard_map/concatenate | solution.py:296
  5.1 10.0 %all-to-all-start = ((f16[16,112,128]{2,1,0:T(8,128)(2,1)}), f16[16,112,128]{2,1,0:T(8,128)(2,1)S(1)}, u32[]{:S(2)}, u32[]{:S(2)}) async-start(f16[16,112,128]{2,1,0:T(8,128)(2,1)} %pad_maximum_fusion), calls=%async_computation | async-start | bytes 917504 | tf_op jit(solution)/shard_map/all_to_all | solution.py:309
  15.1 16.0 %all-to-all-done = f16[16,112,128]{2,1,0:T(8,128)(2,1)S(1)} async-done(((f16[16,112,128]{2,1,0:T(8,128)(2,1)}), f16[16,112,128]{2,1,0:T(8,128)(2,1)S(1)}, u32[]{:S(2)}, u32[]{:S(2)}) %all-to-all-start) | async-done | bytes 458784 | tf_op jit(solution)/shard_map/all_to_all | solution.py:309
  31.1 0.2 broadcast_select_fusion.2
  31.2 1.3 %collective-permute-start.1 = (f16[16,80,128]{2,1,0:T(8,128)(2,1)S(1)}, f16[16,80,128]{2,1,0:T(8,128)(2,1)S(1)}, u32[]{:S(2)}, u32[]{:S(2)}) collective-permute-start(f16[16,80,128]{2,1,0:T(8,128)(2,1)S(1)} %get-tuple-element.7), channel_id=1, source_target_pairs={{0,1},{1,0},{2,3},{3,2},{4,5},{5,4},{6,7},{7,6},{8,9},{9,8},{10,11... | collective-permute-start | bytes 983048 | tf_op jit(solution)/shard_map/ppermute | solution.py:314
  32.5 4.3 %collective-permute-start = (f16[16,80,128]{2,1,0:T(8,128)(2,1)S(1)}, f16[16,80,128]{2,1,0:T(8,128)(2,1)S(1)}, u32[]{:S(2)}, u32[]{:S(2)}) collective-permute-start(f16[16,80,128]{2,1,0:T(8,128)(2,1)S(1)} %get-tuple-element.8), channel_id=1, source_target_pairs={{0,15},{1,2},{2,1},{3,4},{4,3},{5,6},{6,5},{7,8},{8,7},{9,10},{10,... | collective-permute-start | bytes 983048 | tf_op jit(solution)/shard_map/ppermute | solution.py:315
  36.8 0.1 bitcast_convert_fusion.own
  36.9 0.0 copy-start
  36.9 0.0 copy-start.1
  36.9 3.5 %collective-permute-done.1 = f16[16,80,128]{2,1,0:T(8,128)(2,1)S(1)} collective-permute-done((f16[16,80,128]{2,1,0:T(8,128)(2,1)S(1)}, f16[16,80,128]{2,1,0:T(8,128)(2,1)S(1)}, u32[]{:S(2)}, u32[]{:S(2)}) %collective-permute-start.1) | collective-permute-done | bytes 327712 | tf_op jit(solution)/shard_map/ppermute | solution.py:314
  40.4 4.5 %collective-permute-done = f16[16,80,128]{2,1,0:T(8,128)(2,1)S(1)} collective-permute-done((f16[16,80,128]{2,1,0:T(8,128)(2,1)S(1)}, f16[16,80,128]{2,1,0:T(8,128)(2,1)S(1)}, u32[]{:S(2)}, u32[]{:S(2)}) %collective-permute-start) | collective-permute-done | bytes 327712 | tf_op jit(solution)/shard_map/ppermute | solution.py:315
  45.0 0.2 broadcast_select_fusion
  45.1 0.1 bitcast_convert_fusion.1
  45.3 0.0 copy-done
  45.3 0.0 copy-done.1
  45.3 29.2 %shard_map.64 = f32[1792,128]{1,0:T(8,128)S(1)} custom-call(f32[1792,128]{1,0:T(8,128)S(1)} %bitcast_convert_fusion.own, f32[1280,128]{1,0:T(8,128)S(1)} %get-tuple-element.15.left, f32[1280,128]{1,0:T(8,128)S(1)} %get-tuple-element.14.right, bf16[896,1024]{1,0:T(8,128)(2,1)S(1)} %copy-done, bf16[1024,384]{1,0:T(8,128)(2,1)S(1)} %copy-done.1), custom_call_target="tpu_custom_call" | custom-call | tf_op jit(solution)/shard_map/pallas_call | solution.py:271
  74.5 0.1 convert_element_type.24
  74.6 19.2 %all_to_all.10 = f16[16,112,128]{2,1,0:T(8,128)(2,1)S(1)} all-to-all(f16[16,112,128]{2,1,0:T(8,128)(2,1)S(1)} %bitcast.27), channel_id=1, replica_groups=mesh['lat'=16,'lon'=16] {'lat'}, dimensions={0} | all-to-all | bytes 917504 | tf_op jit(solution)/shard_map/all_to_all | solution.py:320
  93.8 0.1 copy.17
  93.9 0.1 convert_multiply_fusion
  94.1 0.5 copy.16
  94.6 1.3 %reshape.33 = f32[2,8,32,384]{3,2,1,0:T(8,128)} reshape(f32[16,32,3,128]{3,2,1,0:T(4,128)S(1)} %copy.16) | data formatting | bytes 1572864 | tf_op jit(solution)/shard_map/reshape | solution.py:302
  (6 shorter events, 0.1 us)
Async XLA Ops:
  5.1 26.0 %all-to-all-start = ((f16[16,112,128]{2,1,0:T(8,128)(2,1)}), f16[16,112,128]{2,1,0:T(8,128)(2,1)S(1)}, u32[]{:S(2)}, u32[]{:S(2)}) async-start(f16[16,112,128]{2,1,0:T(8,128)(2,1)} %pad_maximum_fusion), calls=%async_computation | async-start | bytes 917504 | tf_op jit(solution)/shard_map/all_to_all | solution.py:309
  31.2 9.2 %collective-permute-start.1 = (f16[16,80,128]{2,1,0:T(8,128)(2,1)S(1)}, f16[16,80,128]{2,1,0:T(8,128)(2,1)S(1)}, u32[]{:S(2)}, u32[]{:S(2)}) collective-permute-start(f16[16,80,128]{2,1,0:T(8,128)(2,1)S(1)} %get-tuple-element.7), channel_id=1, source_target_pairs={{0,1},{1,0},{2,3},{3,2},{4,5},{5,4},{6,7},{7,6},{8,9},{9,8},{10,11... | collective-permute-start | bytes 983048 | tf_op jit(solution)/shard_map/ppermute | solution.py:314
  32.5 12.4 %collective-permute-start = (f16[16,80,128]{2,1,0:T(8,128)(2,1)S(1)}, f16[16,80,128]{2,1,0:T(8,128)(2,1)S(1)}, u32[]{:S(2)}, u32[]{:S(2)}) collective-permute-start(f16[16,80,128]{2,1,0:T(8,128)(2,1)S(1)} %get-tuple-element.8), channel_id=1, source_target_pairs={{0,15},{1,2},{2,1},{3,4},{4,3},{5,6},{6,5},{7,8},{8,7},{9,10},{10,... | collective-permute-start | bytes 983048 | tf_op jit(solution)/shard_map/ppermute | solution.py:315
  36.9 8.4 %copy-start = (bf16[896,1024]{1,0:T(8,128)(2,1)S(1)}, bf16[896,1024]{1,0:T(8,128)(2,1)}, u32[]{:S(2)}) copy-start(bf16[896,1024]{1,0:T(8,128)(2,1)} %constant.35.clone.spread) | copy-start | bytes 5505028
  36.9 8.4 %copy-start.1 = (bf16[1024,384]{1,0:T(8,128)(2,1)S(1)}, bf16[1024,384]{1,0:T(8,128)(2,1)}, u32[]{:S(2)}) copy-start(bf16[1024,384]{1,0:T(8,128)(2,1)} %constant.36.clone.collect) | copy-start | bytes 2359300
where the time goes:
time: 96.4 us; the launch traced here: 95.9 us
  Pallas kernels  29.2 us (30%)
  waiting for transfers between devices  24 us (25%)
  blocking collectives  19.2 us (20%)
  starting transfers between devices  15.5 us (16%)
  other arithmetic  3.71 us (4%)
  local copies, waits for them, and re-layouts  2.79 us (3%)
  between operations  1.42 us (1%)
    pallas_call x1, Pallas kernels, core(): pl.pallas_call(kernel, out_shape=jax.ShapeDtypeStruct((16 * OWN_ROWS, 128...  29.2 us
    all_to_all x1, blocking collectives, local(): return unpack(lax.all_to_all(done, 'lat', 0, 0, tiled=True))  19.2 us
    all_to_all x1, waiting for transfers between devices, local(): held = lax.all_to_all(mine, 'lat', 0, 0, tiled=True)  16 us
    all_to_all x1, starting transfers between devices, local(): held = lax.all_to_all(mine, 'lat', 0, 0, tiled=True)  9.98 us
    ppermute x1, waiting for transfers between devices, local(): got1 = lax.ppermute(jnp.where(even, to_left, to_right), 'lon', pairs1)  4.52 us
    ppermute x1, starting transfers between devices, local(): got1 = lax.ppermute(jnp.where(even, to_left, to_right), 'lon', pairs1)  4.27 us
    ppermute x1, waiting for transfers between devices, local(): got0 = lax.ppermute(jnp.where(even, to_right, to_left), 'lon', pairs0)  3.53 us
  transfers between devices with their start and end apart: 3, of which 3 were waited for; matrix products, arithmetic and copies ran while one was open for 0% of the time, Pallas kernels for 0%

commit v1 on v0

v1 whole, which is shorter than its diff:
```python
import functools

import jax
import jax.numpy as jnp
import ml_dtypes
import numpy as np
from jax import lax
from jax.experimental import pallas as pl
from jax.experimental.pallas import tpu as pltpu
from jax.sharding import PartitionSpec as P

CLAT = 32
GRIDS = 5
OMEGA = 0.8
CYCLES = 2
ROWS = 64
PHASES = 8
LEAD = 40
IN_EXP = 14.0
GAIN_EXP = 13.0
OWN_ROWS = 112
HALO_ROWS = 64

f32 = jnp.float32
bf16 = jnp.bfloat16


def column_of(n):
    return 8 * (n % 128 - LEAD) + n // 128


def spread_table():
    columns = column_of(np.arange(1024))
    return (np.arange(896)[:, None] - 256 == columns[None, :]).astype(ml_dtypes.bfloat16)


def collect_table():
    columns = column_of(np.arange(1024))
    return (columns[:, None] == np.arange(384)[None, :]).astype(ml_dtypes.bfloat16)


def centre(level):
    return 4.0 + 4.0**level * 0.25 / (CLAT * CLAT)


def west(v, hop):
    first = pltpu.roll(v[-1], hop, 1)[None]
    return jnp.concatenate([first, v[:-1]], 0) if v.shape[0] > 1 else first


def east(v, hop):
    last = pltpu.roll(v[0], 128 - hop, 1)[None]
    return jnp.concatenate([v[1:], last], 0) if v.shape[0] > 1 else last


def above_first(v):
    lanes = lax.broadcasted_iota(jnp.int32, (8, 128), 0)
    return jnp.stack([jnp.where(lanes > 0, pltpu.roll(v[p], 1, 0), 0.0) for p in range(v.shape[0])])


def below_last(v):
    lanes = lax.broadcasted_iota(jnp.int32, (8, 128), 0)
    return jnp.stack([jnp.where(lanes < 7, pltpu.roll(v[p], 7, 0), 0.0) for p in range(v.shape[0])])


def doubled(v, phases):
    if v.shape[0] == phases:
        return v
    return jnp.concatenate([v[p // 2][None] for p in range(phases)], 0)


def loop(count, body, carry, unroll):
    if unroll >= count:
        for step in range(count):
            carry = body(step, carry)
        return carry
    return lax.fori_loop(0, count, body, carry, unroll=unroll)


def shape_of(level):
    return ROWS >> level, max(PHASES >> level, 1), (2 if level == GRIDS - 1 else 1)


UNROLL = (16, 16, 8, 4, 2)


def sweep(level, x, b, start=False, coarse=None):
    rows, phases, hop = shape_of(level)
    gain = OMEGA / centre(level)
    if start:
        old = lambda r, s: b[r]
    elif coarse is not None:
        old = lambda r, s: x[r] + doubled(coarse[s], phases)
    else:
        old = lambda r, s: x[r]
    first = old(0, 0)
    top = above_first(old(rows - 1, rows // 2 - 1))
    if not start:
        x[rows] = below_last(first)

    def step(r, above, here, below):
        near = (above + below) + (west(here, hop) + east(here, hop))
        if start:
            return (1.2 * gain) * here + (gain * gain) * near
        return 0.2 * here + gain * (b[r] + near)

    def body(s, carry):
        prev, c0 = carry
        c1 = old(2 * s + 1, s)
        n = old(2 * s + 2, s + 1)
        x[2 * s] = step(2 * s, prev, c0, c1)
        x[2 * s + 1] = step(2 * s + 1, c0, c1, n)
        return c1, n

    loop(rows // 2, body, (top, first), UNROLL[level])


def residual(level, x, b, out):
    rows, phases, hop = shape_of(level)
    weight = 2.0 - centre(level)
    first = x[0]
    top = above_first(x[rows - 1])
    x[rows] = below_last(first)
    lane = lax.broadcasted_iota(jnp.int32, (8, 128), 1)

    def across(v):
        if phases > 1:
            return jnp.concatenate([(v[2 * p] + v[2 * p + 1])[None] for p in range(phases // 2)], 0)
        return v + jnp.where(lane % 2 == 0, pltpu.roll(v[0], 127, 1), pltpu.roll(v[0], 1, 1))[None]

    def sides(v):
        if phases > 1:
            to_west = jnp.concatenate([pltpu.roll(v[-1], 1, 1)[None]] + [v[2 * p - 1][None] for p in range(1, phases // 2)], 0)
            to_east = jnp.concatenate([v[2 * p][None] for p in range(1, phases // 2)] + [pltpu.roll(v[0], 127, 1)[None]], 0)
            return to_west + to_east
        near = jnp.where(lane % 2 == 0, pltpu.roll(v[0], 1, 1), pltpu.roll(v[0], 127, 1))
        far = jnp.where(lane % 2 == 0, pltpu.roll(v[0], 126, 1), pltpu.roll(v[0], 2, 1))
        return (near + far)[None]

    def body(s, carry):
        prev, c0 = carry
        c1 = x[2 * s + 1]
        n = x[2 * s + 2]
        flat_n = across(n)
        pair = c0 + c1
        out[s] = across(b[2 * s] + b[2 * s + 1]) + weight * across(pair) + ((prev + flat_n) + sides(pair))
        return across(c1), n

    loop(rows // 2, body, (across(top), first), UNROLL[level])
    out[rows // 2] = below_last(out[0])


def vcycle(level, x, b, fresh):
    rows = shape_of(level)[0]
    if level == GRIDS - 1:
        sweep(level, x[level], b[level], start=True)
        sweep(level, x[level], b[level])
    else:
        if fresh:
            sweep(level, x[level], b[level], start=True)
        else:
            sweep(level, x[level], b[level])
            sweep(level, x[level], b[level])
        residual(level, x[level], b[level], b[level + 1])
        vcycle(level + 1, x, b, True)
        sweep(level, x[level], b[level], coarse=x[level + 1])
    sweep(level, x[level], b[level])
    if level > 0:
        x[level][rows] = jnp.zeros(x[level].shape[1:], f32)


def hat(position, index):
    return jnp.maximum(1.0 - jnp.abs(position - index), 0.0)


def own_number(ref, height, at, lane):
    return [ref[pl.ds(height * half + at, 8, stride=2 * height), :][:, lane : lane + 1] for half in range(2)]


def spread_rows(split, sources, width):
    slot = lax.broadcasted_iota(jnp.int32, (8, 128), 1) // 32

    def put(j, s, pair):
        block = jnp.concatenate(pair, 0)
        high = block.astype(bf16)
        split[16 * s : 16 * s + 16, 128 * j : 128 * j + 128] = high
        split[16 * s : 16 * s + 16, width + 128 * j : width + 128 * j + 128] = (block - high.astype(f32)).astype(bf16)

    for j, (ref, height, units, number, outer) in enumerate(sources):
        scale = [jnp.exp2(k - IN_EXP) for k in own_number(ref, height, *number)]
        for half in range(2):
            rows = {}
            for a in range(16):
                get = lambda at: ref[pl.ds(height * half + at + a, 8, stride=2 * height), :] * scale[half]
                if outer:
                    one, two = get(units[0]), get(units[1])
                    rows[a] = jnp.where(slot % 2 == 0, one, two)
                    rows[a + 16] = jnp.where(slot % 2 == 0, two, one)
                else:
                    middle = get(units[1])
                    low = jnp.where((slot == 1) | (slot == 2), middle, 0.0)
                    high = jnp.where(slot == 1, pltpu.roll(middle, 32, 1), jnp.where(slot == 2, pltpu.roll(middle, 96, 1), 0.0))
                    if units[0] is not None:
                        one = get(units[0])
                        low = jnp.where(slot == 0, one, low)
                        high = jnp.where(slot == 0, pltpu.roll(one, 96, 1), high)
                    if units[2] is not None:
                        two = get(units[2])
                        low = jnp.where(slot == 3, two, low)
                        high = jnp.where(slot == 3, pltpu.roll(two, 32, 1), high)
                    rows[a] = low
                    rows[a + 16] = high
            for s in range(16):
                put(j, 16 * half + s, (rows[2 * s], rows[2 * s + 1]))


OWN_NUMBER = (32, 127)
RIGHT_NUMBER = (32, 127)
LEFT_NUMBER = (16, 2)


def row_winds(row_table, low, high):
    lane = lax.broadcasted_iota(jnp.int32, (8, 128), 1)
    both = []
    for offset in (0, 8):
        rows = []
        for i in range(16):
            parts = []
            for ref, height, at, number in (low, high):
                first = i * height + at
                number_row = i * height + number[0]
                scale = jnp.exp2(ref[number_row : number_row + 1, number[1] : number[1] + 1] - IN_EXP)
                parts.append(ref[first + offset : first + offset + 8, :] * scale)
            rows.append(jnp.where(lane < 64, parts[0], parts[1]))
        both.append(jnp.concatenate(rows, 0))
    table = jnp.concatenate(both, 1).astype(bf16)
    return jnp.dot(row_table, table, preferred_element_type=f32).astype(bf16)


def own_kernel(own, spread, force0, row_table, winds, split):
    spread_rows(
        split,
        (
            (own, OWN_ROWS, (0, 16), OWN_NUMBER, True),
            (own, OWN_ROWS, (32, 48, 64), OWN_NUMBER, False),
            (own, OWN_ROWS, (80, 96), OWN_NUMBER, True),
        ),
        384,
    )
    force0[...] = jnp.dot(split[:, 0:384], spread[...], preferred_element_type=f32) + jnp.dot(
        split[:, 384:768], spread[...], preferred_element_type=f32
    )
    lane = lax.broadcasted_iota(jnp.int32, (8, 128), 1).astype(f32)
    parts = []
    for first in own_number(own, OWN_ROWS, OWN_NUMBER[0], 125):
        for a in range(32):
            parts.append(hat(first + a * 0.25, lane))
    table = jnp.concatenate(parts, 0).astype(bf16)
    row_table[...] = table
    winds[...] = row_winds(table, (own, OWN_ROWS, 64, OWN_NUMBER), (own, OWN_ROWS, 32, OWN_NUMBER))


def kernel(own, left, right, spread, collect, force0, row_table, winds, out, bound, x0, x1, x2, x3, x4, b0, b1, b2, b3, b4, gx, gy, split, flat):
    x = (x0, x1, x2, x3, x4)
    b = (b0, b1, b2, b3, b4)
    spread_rows(
        split,
        (
            (left, HALO_ROWS, (None, 0, 16), LEFT_NUMBER, False),
            (left, HALO_ROWS, (32, 48), LEFT_NUMBER, True),
            (right, HALO_ROWS, (0, 16), RIGHT_NUMBER, True),
            (right, HALO_ROWS, (32, 48, None), RIGHT_NUMBER, False),
        ),
        512,
    )
    n = lax.broadcasted_iota(jnp.int32, (1, 1024), 1)
    column = 8 * ((n & 127) - LEAD) + (n >> 7)

    def shift_of(ref, at, lane):
        first = ref[at : at + 1, lane : lane + 1]
        return first - 96.0 * jnp.floor((first + 48.0) * (1.0 / 96.0))

    shifts = (shift_of(left, 16, 1), shift_of(own, 32, 126), shift_of(right, 32, 126))

    def place(c):
        return c.astype(f32) * 0.25 + 96.0 + jnp.where(c < 0, shifts[0], jnp.where(c < 384, shifts[1], shifts[2]))

    m = lax.broadcasted_iota(jnp.int32, (256, 1), 0)
    lane = m & 127
    spot = jnp.where(lane < 64, lane + 32, lane - 64) + jnp.where(m < 128, 96, jnp.where(lane < 64, 0, 192))
    void = (lane >= 125) | (lane < jnp.where(m < 128, 29, 3))
    index = jnp.where(void, -100000, spot).astype(f32)
    slope = (2.0 * (hat(place(column + 1), index) - hat(place(column - 1), index))).astype(bf16)
    value = (2.0 * hat(place(column), index)).astype(bf16)
    sides = row_winds(row_table[...], (left, HALO_ROWS, 16, LEFT_NUMBER), (right, HALO_ROWS, 32, RIGHT_NUMBER))
    wx = jnp.concatenate([winds[:, 0:128], sides[:, 0:128]], 1)
    wy = jnp.concatenate([winds[:, 128:256], sides[:, 128:256]], 1)
    gx[...] = (
        jnp.dot(split[0:512, 0:512], spread[...], preferred_element_type=f32)
        + jnp.dot(split[0:512, 512:1024], spread[...], preferred_element_type=f32)
        + jnp.dot(wx, slope, preferred_element_type=f32)
    )
    gy[...] = jnp.dot(wy, value, preferred_element_type=f32)

    def cut(ref, r):
        return jnp.stack([ref[8 * r : 8 * r + 8, 128 * p : 128 * p + 128] for p in range(PHASES)])

    first = cut(gy, 0)
    above, here = above_first(cut(gy, ROWS - 1)), first
    for r in range(ROWS):
        below = cut(gy, r + 1) if r < ROWS - 1 else below_last(first)
        b0[r] = cut(force0, r) + cut(gx, r) + (below - above)
        above, here = here, below
    b0[ROWS] = below_last(b0[0])

    for cycle in range(CYCLES):
        vcycle(0, x, b, cycle == 0)

    powers = own_number(own, OWN_ROWS, *OWN_NUMBER) + own_number(left, HALO_ROWS, *LEFT_NUMBER) + own_number(right, HALO_ROWS, *RIGHT_NUMBER)
    power = jnp.max(functools.reduce(jnp.maximum, powers), axis=0, keepdims=True) + (GAIN_EXP - IN_EXP)
    bound[...] = jnp.broadcast_to(jnp.exp2(power), (512, 384))
    scale = jnp.exp2(-power)
    for s in range(ROWS // 2):
        pair = jnp.concatenate([x0[2 * s], x0[2 * s + 1]], 1) * scale
        high = pair.astype(bf16)
        low = (pair - high.astype(f32)).astype(bf16)
        for p in range(PHASES):
            split[16 * s : 16 * s + 16, 128 * p : 128 * p + 128] = high[p]
            split[512 + 16 * s : 528 + 16 * s, 128 * p : 128 * p + 128] = low[p]
    block = jnp.dot(split[0:512, :], collect[...], preferred_element_type=f32) + jnp.dot(
        split[512:1024, :], collect[...], preferred_element_type=f32
    )
    for j in range(3):
        for r in range(ROWS):
            flat[pl.ds(512 * j + r, 8, stride=64), :] = block[8 * r : 8 * r + 8, 128 * j : 128 * j + 128]
    for j in range(3):
        out[:, 128 * j : 128 * j + 128] = flat[512 * j : 512 * j + 512, :]


PARAMS = dict(compiler_params=pltpu.CompilerParams(vmem_limit_bytes=40 * 1024 * 1024))


def core_own(own, interpret=False):
    return pl.pallas_call(
        own_kernel,
        out_shape=(
            jax.ShapeDtypeStruct((512, 1024), f32),
            jax.ShapeDtypeStruct((512, 128), bf16),
            jax.ShapeDtypeStruct((512, 256), bf16),
        ),
        scratch_shapes=[pltpu.VMEM((512, 768), bf16)],
        interpret=interpret,
        **PARAMS,
    )(own, jnp.asarray(spread_table()[256:640]))


def core(own, left, right, parts, interpret=False):
    grids = []
    for level in range(GRIDS):
        rows, phases, _ = shape_of(level)
        grids.append(pltpu.VMEM((rows + 1, phases, 8, 128), f32))
    table = spread_table()
    return pl.pallas_call(
        kernel,
        out_shape=(jax.ShapeDtypeStruct((512, 384), f32), jax.ShapeDtypeStruct((512, 384), f32)),
        scratch_shapes=grids
        + grids
        + [
            pltpu.VMEM((512, 1024), f32),
            pltpu.VMEM((512, 1024), f32),
            pltpu.VMEM((1024, 1024), bf16),
            pltpu.VMEM((1536, 128), f32),
        ],
        interpret=interpret,
        **PARAMS,
    )(own, left, right, jnp.asarray(np.concatenate([table[0:256], table[640:896]])), jnp.asarray(collect_table()), *parts)


def parcel_kernel(lat_first, lon_first, increments_hbm, winds_hbm, out, increments, ens_winds, sems):
    copies = [
        pltpu.make_async_copy(increments_hbm, increments, sems.at[0]),
        pltpu.make_async_copy(winds_hbm, ens_winds, sems.at[1]),
    ]
    for copy in copies:
        copy.start()
    for copy in copies:
        copy.wait()
    top = jnp.max(jnp.max(jnp.abs(increments[...]), axis=(0, 1)), axis=(0, 1), keepdims=True)
    gust = jnp.max(jnp.max(jnp.abs(ens_winds[...].astype(f32)), axis=(0, 1)), axis=(0, 1), keepdims=True)
    top = jnp.maximum(jnp.maximum(top, 8.0 * gust), 1e-30)
    power = jnp.ceil(jnp.log2(top))
    scale = jnp.exp2(IN_EXP - power)
    lat, lon = lat_first[0].astype(f32), lon_first[0].astype(f32)
    lane = lax.broadcasted_iota(jnp.int32, (16, 128), 1)
    slot = lane // 32
    even = slot % 2 == 0
    for field in range(2):
        for k in range(8):
            d = 8 * field + k
            block = increments[field, k] * scale
            low, high = block[0:16], block[16:32]
            for at, c in ((0, 0), (80, 256)):
                out[d, at : at + 16, :] = jnp.where(even, low[:, c : c + 128], high[:, c : c + 128])
                out[d, at + 16 : at + 32, :] = jnp.where(even, high[:, c : c + 128], low[:, c : c + 128])
            low, high = low[:, 128:256], high[:, 128:256]
            on, back = pltpu.roll(high, 32, 1), pltpu.roll(high, 96, 1)
            u, v = ens_winds[0, k].astype(f32) * scale, ens_winds[1, k].astype(f32) * scale
            across, along = (v, -u) if field == 0 else (u, v)
            winds = jnp.concatenate([across, along], 0)
            winds = jnp.concatenate([winds, jnp.zeros((16, 32), f32)], 1)
            first = jnp.where(slot == 0, low, jnp.where(slot == 1, on, pltpu.roll(winds, 64, 1)))
            first = jnp.where(lane == 125, lat, jnp.where(lane == 126, lon, jnp.where(lane == 127, power, first)))
            last = jnp.where(slot == 3, low, jnp.where(slot == 2, back, pltpu.roll(winds, 96, 1)))
            last = jnp.where(lane == 0, lat, jnp.where(lane == 1, lon, jnp.where(lane == 2, power, last)))
            out[d, 32:48, :] = first
            out[d, 48:64, :] = jnp.where(slot == 0, back, jnp.where(slot == 3, on, low))
            out[d, 64:80, :] = last


def in_hbm(value):
    return pltpu.with_memory_space_constraint(value, pltpu.HBM)


def parcel(increments, ens_winds, lat_offsets, lon_offsets, interpret=False):
    scalar = pl.BlockSpec(memory_space=pltpu.SMEM)
    whole = pl.BlockSpec(memory_space=pltpu.HBM)
    return pl.pallas_call(
        parcel_kernel,
        out_shape=jax.ShapeDtypeStruct((16, OWN_ROWS, 128), f32),
        in_specs=[scalar, scalar, whole, whole],
        scratch_shapes=[
            pltpu.VMEM(increments.shape, f32),
            pltpu.VMEM(ens_winds.shape, bf16),
            pltpu.SemaphoreType.DMA((2,)),
        ],
        interpret=interpret,
        **PARAMS,
    )(lat_offsets, lon_offsets, in_hbm(increments), in_hbm(ens_winds))


def local(increments, ens_winds, lat_offsets, lon_offsets):
    count = lax.axis_size("lon")
    mine = parcel(increments, ens_winds, lat_offsets, lon_offsets).astype(jnp.float16)
    held, me = lax.optimization_barrier((lax.all_to_all(mine, "lat", 0, 0, tiled=True), lax.axis_index("lon")))
    even = me % 2 == 0
    to_left, to_right = held[:, 0:HALO_ROWS], held[:, OWN_ROWS - HALO_ROWS :]
    pairs0 = [(i, i ^ 1) for i in range(count)]
    pairs1 = [(i, (((i - 1) ^ 1) + 1) % count) for i in range(count)]
    got0 = lax.ppermute(jnp.where(even, to_right, to_left), "lon", pairs0)
    got1 = lax.ppermute(jnp.where(even, to_left, to_right), "lon", pairs1)
    own = held.astype(f32).reshape(16 * OWN_ROWS, 128)
    parts = core_own(own)
    left = jnp.where(even, got1, got0).astype(f32).reshape(16 * HALO_ROWS, 128)
    right = jnp.where(even, got0, got1).astype(f32).reshape(16 * HALO_ROWS, 128)
    done, bound = core(own, left, right, parts)
    back = lax.all_to_all(done.astype(jnp.float16).reshape(16, 32, 384), "lat", 0, 0, tiled=True)
    return (back.astype(f32) * bound.reshape(back.shape)).reshape(increments.shape)


def solution(mesh):
    in_specs = (P(None, None, "lat", "lon"), P(None, None, "lat", "lon"), P("lat"), P("lon"))
    out_specs = P(None, None, "lat", "lon")
    return jax.shard_map(local, mesh=mesh, in_specs=in_specs, out_specs=out_specs, check_vma=False)
```

time: 96.4 us -> 73.9 us (0.77)
  Pallas kernels: 29.2 us -> 15.8 us
  waiting for transfers between devices: 24 us -> 20.7 us
  local copies, waits for them, and re-layouts: 2.79 us -> 0.02 us
  blocking collectives: 19.2 us -> 17.8 us
  other arithmetic: 3.71 us -> 2.35 us
    pallas_call x1 -> x3, Pallas kernels: 29.2 us -> 15.8 us  [the longest x1 12.4 us: core(): pl.pallas_call(kernel, out_shape=(jax.ShapeDtypeStruct((512, 384), f32),...]
    ppermute x1, waiting for transfers between devices: 3.53 us -> 0.26 us  [local(): got0 = lax.ppermute(jnp.where(even, to_right, to_left), 'lon', pairs0)]
    all_to_all x1, blocking collectives: 19.2 us -> 17.8 us  [local(): lax.all_to_all(done.astype(jnp.float16).reshape(16, 32, 384), 'lat', 0, 0...]
    reshape x1 -> x0, local copies, waits for them, and re-layouts: 1.3 us -> none  [unpack(): values.reshape(16, 3, 32, 128).transpose(0, 2, 1, 3).reshape(2, 8, 32, 384)]
    another operation x3 -> x0, other arithmetic: 1.25 us -> none
    concatenate x1 -> x0, other arithmetic: 0.96 us -> none  [parcel(): jnp.concatenate([inc[:, :, 0:128], inc[:, :, 128:256], winds, inc[:, :, 2...]
  transfers between devices with their start and end apart: 3 -> 3, of which waited for: 3 -> 3; matrix products, arithmetic and copies ran while one was open for 0% -> 0% of each run, Pallas kernels for 0% -> 3%
where the time goes in v1:
time: 73.9 us; the launch traced here: 73.7 us
  waiting for transfers between devices  20.7 us (28%)
  blocking collectives  17.8 us (24%)
  Pallas kernels  15.8 us (21%)
  starting transfers between devices  15.5 us (21%)
  other arithmetic  2.35 us (3%)
  between operations  1.4 us (2%)
    all_to_all x1, blocking collectives, local(): lax.all_to_all(done.astype(jnp.float16).reshape(16, 32, 384), 'lat', 0, 0...  17.8 us
    all_to_all x1, waiting for transfers between devices, local(): lax.all_to_all(mine, 'lat', 0, 0, tiled=True)  16 us
    pallas_call x1, Pallas kernels, core(): pl.pallas_call(kernel, out_shape=(jax.ShapeDtypeStruct((512, 384), f32),...  12.4 us
    all_to_all x1, starting transfers between devices, local(): lax.all_to_all(mine, 'lat', 0, 0, tiled=True)  9.98 us
    ppermute x1, waiting for transfers between devices, local(): got1 = lax.ppermute(jnp.where(even, to_left, to_right), 'lon', pairs1)  4.52 us
    ppermute x1, starting transfers between devices, local(): got1 = lax.ppermute(jnp.where(even, to_left, to_right), 'lon', pairs1)  4.27 us
    pallas_call x1, Pallas kernels, core_own(): pl.pallas_call(own_kernel, out_shape=(jax.ShapeDtypeStruct((512, 1024), f...  1.85 us
    pallas_call x1, Pallas kernels, parcel(): pl.pallas_call(parcel_kernel, out_shape=jax.ShapeDtypeStruct((16, OWN_ROW...  1.6 us
  transfers between devices with their start and end apart: 3, of which 3 were waited for; matrix products, arithmetic and copies ran while one was open for 0% of the time, Pallas kernels for 3%

profile of v1, /device:TPU:1, one launch (start us, length us, event | category | flops | bytes accessed | tf_op | source)
XLA Modules:
  0.0 73.7 jit_solution(5571524279976818290)
XLA Ops:
  1.3 1.6 %shard_map.73 = f32[16,112,128]{2,1,0:T(8,128)S(1)} custom-call(s32[1]{0:T(128)S(6)} %copy.8.lat_first, s32[1]{0:T(128)S(6)} %copy.9.lon_first, f32[2,8,32,384]{3,2,1,0:T(8,128)} %increments_hbm.1, bf16[2,8,8,96]{3,2,1,0:T(8,128)(2,1)} %winds_hbm.1), custom_call_target="tpu_custom_call" | custom-call | tf_op jit(solution)/shard_map/pallas_call | solution.py:427
  2.9 0.0 copy-start.2
  2.9 0.8 %convert_element_type.12 = f16[16,112,128]{2,1,0:T(8,128)(2,1)} convert(f32[16,112,128]{2,1,0:T(8,128)S(1)} %shard_map.73) | non-fusion elementwise | flops 229376 | bytes 1376256 | tf_op jit(solution)/shard_map/convert_element_type | solution.py:443
  3.7 10.0 %all-to-all-start = ((f16[16,112,128]{2,1,0:T(8,128)(2,1)}), f16[16,112,128]{2,1,0:T(8,128)(2,1)S(1)}, u32[]{:S(2)}, u32[]{:S(2)}) async-start(f16[16,112,128]{2,1,0:T(8,128)(2,1)} %convert_element_type.12), calls=%async_computation | async-start | bytes 917504 | tf_op jit(solution)/shard_map/all_to_all | solution.py:444
  13.7 16.0 %all-to-all-done = f16[16,112,128]{2,1,0:T(8,128)(2,1)S(1)} async-done(((f16[16,112,128]{2,1,0:T(8,128)(2,1)}), f16[16,112,128]{2,1,0:T(8,128)(2,1)S(1)}, u32[]{:S(2)}, u32[]{:S(2)}) %all-to-all-start) | async-done | bytes 458784 | tf_op jit(solution)/shard_map/all_to_all | solution.py:444
  29.7 0.2 broadcast_select_fusion.2
  29.9 1.3 %collective-permute-start.1 = (f16[16,64,128]{2,1,0:T(8,128)(2,1)S(1)}, f16[16,64,128]{2,1,0:T(8,128)(2,1)S(1)}, u32[]{:S(2)}, u32[]{:S(2)}) collective-permute-start(f16[16,64,128]{2,1,0:T(8,128)(2,1)S(1)} %get-tuple-element.21), channel_id=1, source_target_pairs={{0,1},{1,0},{2,3},{3,2},{4,5},{5,4},{6,7},{7,6},{8,9},{9,8},{10,11... | collective-permute-start | bytes 786440 | tf_op jit(solution)/shard_map/ppermute | solution.py:449
  31.2 4.3 %collective-permute-start = (f16[16,64,128]{2,1,0:T(8,128)(2,1)S(1)}, f16[16,64,128]{2,1,0:T(8,128)(2,1)S(1)}, u32[]{:S(2)}, u32[]{:S(2)}) collective-permute-start(f16[16,64,128]{2,1,0:T(8,128)(2,1)S(1)} %get-tuple-element.22), channel_id=1, source_target_pairs={{0,15},{1,2},{2,1},{3,4},{4,3},{5,6},{6,5},{7,8},{8,7},{9,10},{10,... | collective-permute-start | bytes 786440 | tf_op jit(solution)/shard_map/ppermute | solution.py:450
  35.4 0.1 bitcast_convert_fusion.own
  35.5 0.0 copy-done.2
  35.5 0.0 copy-start
  35.5 0.0 copy-start.1
  35.6 1.8 %shard_map.74 = (f32[512,1024]{1,0:T(8,128)S(1)}, bf16[512,128]{1,0:T(8,128)(2,1)S(1)}, bf16[512,256]{1,0:T(8,128)(2,1)S(1)}) custom-call(f32[1792,128]{1,0:T(8,128)S(1)} %bitcast_convert_fusion.own, bf16[384,1024]{1,0:T(8,128)(2,1)S(1)} %copy-done.2), custom_call_target="tpu_custom_call" | custom-call | tf_op jit(solution)/shard_map/pallas_call | solution.py:344
  37.4 0.3 collective-permute-done.1
  37.7 4.5 %collective-permute-done = f16[16,64,128]{2,1,0:T(8,128)(2,1)S(1)} collective-permute-done((f16[16,64,128]{2,1,0:T(8,128)(2,1)S(1)}, f16[16,64,128]{2,1,0:T(8,128)(2,1)S(1)}, u32[]{:S(2)}, u32[]{:S(2)}) %collective-permute-start) | collective-permute-done | bytes 262176 | tf_op jit(solution)/shard_map/ppermute | solution.py:450
  42.2 0.2 broadcast_select_fusion
  42.4 0.1 bitcast_convert_fusion.1
  42.5 0.0 copy-done
  42.5 0.0 copy-done.1
  42.5 12.4 %shard_map.75 = (f32[512,384]{1,0:T(8,128)S(1)}, f32[512,384]{1,0:T(8,128)S(1)}) custom-call(f32[1792,128]{1,0:T(8,128)S(1)} %bitcast_convert_fusion.own, f32[1024,128]{1,0:T(8,128)S(1)} %get-tuple-element.24.left, f32[1024,128]{1,0:T(8,128)S(1)} %get-tuple-element.23.right, bf16[512,1024]{1,0:T(8,128)(2,1)S(1)} %copy-done, bf16[1024,384]{1,0:T(8,128)(2,1)S(1)} %copy-done.1, ...), custom_call_target="tpu_custom_call" | custom-call | tf_op jit(solution)/shard_map/pallas_call | solution.py:363
  54.8 0.1 convert_element_type.13
  54.9 17.8 %all_to_all.10 = f16[16,32,384]{2,1,0:T(8,128)(2,1)S(1)} all-to-all(f16[16,32,384]{2,1,0:T(8,128)(2,1)S(1)} %bitcast.13), channel_id=1, replica_groups=mesh['lat'=16,'lon'=16] {'lat'}, dimensions={0} | all-to-all | bytes 786432 | tf_op jit(solution)/shard_map/all_to_all | solution.py:456
  72.7 1.0 %convert_multiply_fusion = f32[16,32,384]{2,1,0:T(8,128)} fusion(f32[16,32,384]{2,1,0:T(8,128)S(1)} %bitcast.12, f16[16,32,384]{2,1,0:T(8,128)(2,1)S(1)} %all_to_all.10), kind=kLoop, calls=%fused_computation | loop fusion | flops 393216 | bytes 1966080 | tf_op jit(solution)/shard_map/mul | solution.py:457
Async XLA Ops:
  2.9 32.6 %copy-start.2 = (bf16[384,1024]{1,0:T(8,128)(2,1)S(1)}, bf16[384,1024]{1,0:T(8,128)(2,1)}, u32[]{:S(2)}) copy-start(bf16[384,1024]{1,0:T(8,128)(2,1)} %constant.24.clone.spread) | copy-start | bytes 2359300
  3.7 26.0 %all-to-all-start = ((f16[16,112,128]{2,1,0:T(8,128)(2,1)}), f16[16,112,128]{2,1,0:T(8,128)(2,1)S(1)}, u32[]{:S(2)}, u32[]{:S(2)}) async-start(f16[16,112,128]{2,1,0:T(8,128)(2,1)} %convert_element_type.12), calls=%async_computation | async-start | bytes 917504 | tf_op jit(solution)/shard_map/all_to_all | solution.py:444
  29.9 7.8 %collective-permute-start.1 = (f16[16,64,128]{2,1,0:T(8,128)(2,1)S(1)}, f16[16,64,128]{2,1,0:T(8,128)(2,1)S(1)}, u32[]{:S(2)}, u32[]{:S(2)}) collective-permute-start(f16[16,64,128]{2,1,0:T(8,128)(2,1)S(1)} %get-tuple-element.21), channel_id=1, source_target_pairs={{0,1},{1,0},{2,3},{3,2},{4,5},{5,4},{6,7},{7,6},{8,9},{9,8},{10,11... | collective-permute-start | bytes 786440 | tf_op jit(solution)/shard_map/ppermute | solution.py:449
  31.2 11.0 %collective-permute-start = (f16[16,64,128]{2,1,0:T(8,128)(2,1)S(1)}, f16[16,64,128]{2,1,0:T(8,128)(2,1)S(1)}, u32[]{:S(2)}, u32[]{:S(2)}) collective-permute-start(f16[16,64,128]{2,1,0:T(8,128)(2,1)S(1)} %get-tuple-element.22), channel_id=1, source_target_pairs={{0,15},{1,2},{2,1},{3,4},{4,3},{5,6},{6,5},{7,8},{8,7},{9,10},{10,... | collective-permute-start | bytes 786440 | tf_op jit(solution)/shard_map/ppermute | solution.py:450
  35.5 6.9 %copy-start = (bf16[512,1024]{1,0:T(8,128)(2,1)S(1)}, bf16[512,1024]{1,0:T(8,128)(2,1)}, u32[]{:S(2)}) copy-start(bf16[512,1024]{1,0:T(8,128)(2,1)} %constant.25.clone.spread) | copy-start | bytes 3145732
  35.5 6.9 %copy-start.1 = (bf16[1024,384]{1,0:T(8,128)(2,1)S(1)}, bf16[1024,384]{1,0:T(8,128)(2,1)}, u32[]{:S(2)}) copy-start(bf16[1024,384]{1,0:T(8,128)(2,1)} %constant.26.clone.collect) | copy-start | bytes 2359300

commit v2 on v1

--- a/solution.py
+++ b/solution.py
@@ -12,6 +12,7 @@
 CLAT = 32
 GRIDS = 5
 OMEGA = 0.8
+COARSE_SWEEPS = 4
 CYCLES = 2
 ROWS = 64
 PHASES = 8
@@ -35,7 +36,11 @@
 
 
 def collect_table():
-    columns = column_of(np.arange(1024))
+    n = np.arange(512)
+    phase, lane = n // 128, n % 128
+    second = (lane < 24) | (lane >= 104)
+    columns = np.where(second, 8 * ((lane + 64) % 128 - LEAD) + phase + 4, 8 * (lane - LEAD) + phase)
+    columns = np.where(second | ((lane >= LEAD) & (lane < LEAD + 48)), columns, -1)
     return (columns[:, None] == np.arange(384)[None, :]).astype(ml_dtypes.bfloat16)
 
 
@@ -81,7 +86,7 @@
     return ROWS >> level, max(PHASES >> level, 1), (2 if level == GRIDS - 1 else 1)
 
 
-UNROLL = (16, 16, 8, 4, 2)
+UNROLL = (32, 16, 8, 4, 2)
 
 
 def sweep(level, x, b, start=False, coarse=None):
@@ -150,23 +155,41 @@
     out[rows // 2] = below_last(out[0])
 
 
+def coarsest(x, b):
+    level = GRIDS - 1
+    rows, _, hop = shape_of(level)
+    gain = OMEGA / centre(level)
+    source = [b[r][0] for r in range(rows)]
+    sub = lax.broadcasted_iota(jnp.int32, (8, 128), 0)
+    v = source
+    for turn in range(COARSE_SWEEPS - 1):
+        above = [jnp.where(sub > 0, pltpu.roll(v[-1], 1, 0), 0.0)] + v[:-1]
+        below = v[1:] + [jnp.where(sub < 7, pltpu.roll(v[0], 7, 0), 0.0)]
+        near = [(above[r] + below[r]) + (pltpu.roll(v[r], hop, 1) + pltpu.roll(v[r], 128 - hop, 1)) for r in range(rows)]
+        if turn == 0:
+            v = [(1.2 * gain) * v[r] + (gain * gain) * near[r] for r in range(rows)]
+        else:
+            v = [0.2 * v[r] + gain * (source[r] + near[r]) for r in range(rows)]
+    for r in range(rows):
+        x[r] = v[r][None]
+    x[rows] = jnp.zeros(x.shape[1:], f32)
+
+
 def vcycle(level, x, b, fresh):
-    rows = shape_of(level)[0]
     if level == GRIDS - 1:
+        coarsest(x[level], b[level])
+        return
+    if fresh:
         sweep(level, x[level], b[level], start=True)
+    else:
         sweep(level, x[level], b[level])
-    else:
-        if fresh:
-            sweep(level, x[level], b[level], start=True)
-        else:
-            sweep(level, x[level], b[level])
-            sweep(level, x[level], b[level])
-        residual(level, x[level], b[level], b[level + 1])
-        vcycle(level + 1, x, b, True)
-        sweep(level, x[level], b[level], coarse=x[level + 1])
+        sweep(level, x[level], b[level])
+    residual(level, x[level], b[level], b[level + 1])
+    vcycle(level + 1, x, b, True)
+    sweep(level, x[level], b[level], coarse=x[level + 1])
     sweep(level, x[level], b[level])
     if level > 0:
-        x[level][rows] = jnp.zeros(x[level].shape[1:], f32)
+        x[level][shape_of(level)[0]] = jnp.zeros(x[level].shape[1:], f32)
 
 
 def hat(position, index):
@@ -296,8 +319,8 @@
     wx = jnp.concatenate([winds[:, 0:128], sides[:, 0:128]], 1)
     wy = jnp.concatenate([winds[:, 128:256], sides[:, 128:256]], 1)
     gx[...] = (
-        jnp.dot(split[0:512, 0:512], spread[...], preferred_element_type=f32)
-        + jnp.dot(split[0:512, 512:1024], spread[...], preferred_element_type=f32)
+        jnp.dot(split[:, 0:512], spread[...], preferred_element_type=f32)
+        + jnp.dot(split[:, 512:1024], spread[...], preferred_element_type=f32)
         + jnp.dot(wx, slope, preferred_element_type=f32)
     )
     gy[...] = jnp.dot(wy, value, preferred_element_type=f32)
@@ -320,15 +343,17 @@
     power = jnp.max(functools.reduce(jnp.maximum, powers), axis=0, keepdims=True) + (GAIN_EXP - IN_EXP)
     bound[...] = jnp.broadcast_to(jnp.exp2(power), (512, 384))
     scale = jnp.exp2(-power)
+    lane = lax.broadcasted_iota(jnp.int32, (8, 128), 1)
+    inside = (lane >= LEAD) & (lane < LEAD + 48)
     for s in range(ROWS // 2):
-        pair = jnp.concatenate([x0[2 * s], x0[2 * s + 1]], 1) * scale
-        high = pair.astype(bf16)
-        low = (pair - high.astype(f32)).astype(bf16)
-        for p in range(PHASES):
-            split[16 * s : 16 * s + 16, 128 * p : 128 * p + 128] = high[p]
-            split[512 + 16 * s : 528 + 16 * s, 128 * p : 128 * p + 128] = low[p]
-    block = jnp.dot(split[0:512, :], collect[...], preferred_element_type=f32) + jnp.dot(
-        split[512:1024, :], collect[...], preferred_element_type=f32
+        for p in range(PHASES // 2):
+            pair = [jnp.where(inside, x0[r, p], pltpu.roll(x0[r, p + 4], 64, 1)) for r in (2 * s, 2 * s + 1)]
+            pair = jnp.concatenate(pair, 0) * scale
+            high = pair.astype(bf16)
+            split[16 * s : 16 * s + 16, 128 * p : 128 * p + 128] = high
+            split[16 * s : 16 * s + 16, 512 + 128 * p : 640 + 128 * p] = (pair - high.astype(f32)).astype(bf16)
+    block = jnp.dot(split[:, 0:512], collect[...], preferred_element_type=f32) + jnp.dot(
+        split[:, 512:1024], collect[...], preferred_element_type=f32
     )
     for j in range(3):
         for r in range(ROWS):
@@ -368,7 +393,7 @@
         + [
             pltpu.VMEM((512, 1024), f32),
             pltpu.VMEM((512, 1024), f32),
-            pltpu.VMEM((1024, 1024), bf16),
+            pltpu.VMEM((512, 1024), bf16),
             pltpu.VMEM((1536, 128), f32),
         ],
         interpret=interpret,
@@ -376,7 +401,7 @@
     )(own, left, right, jnp.asarray(np.concatenate([table[0:256], table[640:896]])), jnp.asarray(collect_table()), *parts)
 
 
-def parcel_kernel(lat_first, lon_first, increments_hbm, winds_hbm, out, increments, ens_winds, sems):
+def parcel_kernel(lat_first, lon_first, increments_hbm, winds_hbm, out, odd, increments, ens_winds, sems):
     copies = [
         pltpu.make_async_copy(increments_hbm, increments, sems.at[0]),
         pltpu.make_async_copy(winds_hbm, ens_winds, sems.at[1]),
@@ -391,6 +416,7 @@
     power = jnp.ceil(jnp.log2(top))
     scale = jnp.exp2(IN_EXP - power)
     lat, lon = lat_first[0].astype(f32), lon_first[0].astype(f32)
+    odd[...] = jnp.full(odd.shape, ((lon_first[0] + 48) // 96 % 2).astype(f32))
     lane = lax.broadcasted_iota(jnp.int32, (16, 128), 1)
     slot = lane // 32
     even = slot % 2 == 0
@@ -426,7 +452,10 @@
     whole = pl.BlockSpec(memory_space=pltpu.HBM)
     return pl.pallas_call(
         parcel_kernel,
-        out_shape=jax.ShapeDtypeStruct((16, OWN_ROWS, 128), f32),
+        out_shape=(
+            jax.ShapeDtypeStruct((16, OWN_ROWS, 128), f32),
+            jax.ShapeDtypeStruct((16, HALO_ROWS, 128), f32),
+        ),
         in_specs=[scalar, scalar, whole, whole],
         scratch_shapes=[
             pltpu.VMEM(increments.shape, f32),
@@ -440,9 +469,9 @@
 
 def local(increments, ens_winds, lat_offsets, lon_offsets):
     count = lax.axis_size("lon")
-    mine = parcel(increments, ens_winds, lat_offsets, lon_offsets).astype(jnp.float16)
-    held, me = lax.optimization_barrier((lax.all_to_all(mine, "lat", 0, 0, tiled=True), lax.axis_index("lon")))
-    even = me % 2 == 0
+    mine, odd = parcel(increments, ens_winds, lat_offsets, lon_offsets)
+    held = lax.all_to_all(mine.astype(jnp.float16), "lat", 0, 0, tiled=True)
+    even = odd < 0.5
     to_left, to_right = held[:, 0:HALO_ROWS], held[:, OWN_ROWS - HALO_ROWS :]
     pairs0 = [(i, i ^ 1) for i in range(count)]
     pairs1 = [(i, (((i - 1) ^ 1) + 1) % count) for i in range(count)]

time: 73.9 us -> 71.8 us (0.972)
  blocking collectives: 17.8 us -> 43.6 us
  waiting for transfers between devices: 20.7 us -> 5.71 us
  starting transfers between devices: 15.5 us -> 5.02 us
  Pallas kernels: 15.8 us -> 14.2 us
    all_to_all x0 -> x1, blocking collectives: none -> 25.7 us  [local(): held = lax.all_to_all(mine.astype(jnp.float16), 'lat', 0, 0, tiled=True)]
    all_to_all x1 -> x0, waiting for transfers between devices: 16 us -> none  [local(): lax.all_to_all(mine, 'lat', 0, 0, tiled=True)]
    all_to_all x1 -> x0, starting transfers between devices: 9.98 us -> none  [local(): lax.all_to_all(mine, 'lat', 0, 0, tiled=True)]
    pallas_call x1, Pallas kernels: 12.4 us -> 10.7 us  [core(): pl.pallas_call(kernel, out_shape=(jax.ShapeDtypeStruct((512, 384), f32),...]
    ppermute x1, waiting for transfers between devices: 0.26 us -> 1.89 us  [local(): got0 = lax.ppermute(jnp.where(even, to_right, to_left), 'lon', pairs0)]
    ppermute x1, starting transfers between devices: 1.3 us -> 0.01 us  [local(): got0 = lax.ppermute(jnp.where(even, to_right, to_left), 'lon', pairs0)]
    convert_element_type x1, other arithmetic: 0.83 us -> 0.06 us  [local(): held = lax.all_to_all(mine.astype(jnp.float16), 'lat', 0, 0, tiled=True)]
    ppermute x1, starting transfers between devices: 4.27 us -> 5.02 us  [local(): got1 = lax.ppermute(jnp.where(even, to_left, to_right), 'lon', pairs1)]
  transfers between devices with their start and end apart: 3 -> 2, of which waited for: 3 -> 2; matrix products, arithmetic and copies ran while one was open for 0% -> 0% of each run, Pallas kernels for 3% -> 3%
where the time goes in v2:
time: 71.8 us; the launch traced here: 71.7 us
  blocking collectives  43.6 us (61%)
  Pallas kernels  14.2 us (20%)
  waiting for transfers between devices  5.71 us (8%)
  starting transfers between devices  5.02 us (7%)
  other arithmetic  1.73 us (2%)
  between operations  1.4 us (2%)
    all_to_all x1, blocking collectives, local(): held = lax.all_to_all(mine.astype(jnp.float16), 'lat', 0, 0, tiled=True)  25.7 us
    all_to_all x1, blocking collectives, local(): lax.all_to_all(done.astype(jnp.float16).reshape(16, 32, 384), 'lat', 0, 0...  17.8 us
    pallas_call x1, Pallas kernels, core(): pl.pallas_call(kernel, out_shape=(jax.ShapeDtypeStruct((512, 384), f32),...  10.7 us
    ppermute x1, starting transfers between devices, local(): got1 = lax.ppermute(jnp.where(even, to_left, to_right), 'lon', pairs1)  5.02 us
    ppermute x1, waiting for transfers between devices, local(): got1 = lax.ppermute(jnp.where(even, to_left, to_right), 'lon', pairs1)  3.82 us
    ppermute x1, waiting for transfers between devices, local(): got0 = lax.ppermute(jnp.where(even, to_right, to_left), 'lon', pairs0)  1.89 us
    pallas_call x1, Pallas kernels, core_own(): pl.pallas_call(own_kernel, out_shape=(jax.ShapeDtypeStruct((512, 1024), f...  1.86 us
    pallas_call x1, Pallas kernels, parcel(): pl.pallas_call(parcel_kernel, out_shape=(jax.ShapeDtypeStruct((16, OWN_RO...  1.63 us
  transfers between devices with their start and end apart: 2, of which 2 were waited for; matrix products, arithmetic and copies ran while one was open for 0% of the time, Pallas kernels for 3%

profile of v2, /device:TPU:1, one launch (start us, length us, event | category | flops | bytes accessed | tf_op | source)
XLA Modules:
  0.0 71.7 jit_solution(16536635927091130839)
XLA Ops:
  1.3 1.6 %shard_map.73 = (f32[16,112,128]{2,1,0:T(8,128)S(1)}, f32[16,64,128]{2,1,0:T(8,128)S(1)}) custom-call(s32[1]{0:T(128)S(6)} %copy.8.lat_first, s32[1]{0:T(128)S(6)} %copy.9.lon_first, f32[2,8,32,384]{3,2,1,0:T(8,128)} %increments_hbm.1, bf16[2,8,8,96]{3,2,1,0:T(8,128)(2,1)} %winds_hbm.1), custom_call_target="tpu_custom_call" | custom-call | tf_op jit(solution)/shard_map/pallas_call | solution.py:453
  2.9 0.1 convert_element_type.12
  3.0 25.7 %all_to_all.10 = f16[16,112,128]{2,1,0:T(8,128)(2,1)S(1)} all-to-all(f16[16,112,128]{2,1,0:T(8,128)(2,1)S(1)} %convert_element_type.12), channel_id=1, replica_groups=mesh['lat'=16,'lon'=16] {'lat'}, dimensions={0} | all-to-all | bytes 917504 | tf_op jit(solution)/shard_map/all_to_all | solution.py:473
  28.8 0.0 copy-start.1
  28.8 0.2 slice_select_fusion
  28.9 0.1 slice_select_fusion.1
  29.0 5.0 %collective-permute-start = (f16[16,64,128]{2,1,0:T(8,128)(2,1)S(1)}, f16[16,64,128]{2,1,0:T(8,128)(2,1)S(1)}, u32[]{:S(2)}, u32[]{:S(2)}) collective-permute-start(f16[16,64,128]{2,1,0:T(8,128)(2,1)S(1)} %slice_select_fusion.1), channel_id=1, source_target_pairs={{0,15},{1,2},{2,1},{3,4},{4,3},{5,6},{6,5},{7,8},{8,7},{9,10},{10,... | collective-permute-start | bytes 786440 | tf_op jit(solution)/shard_map/ppermute | solution.py:479
  34.1 0.0 collective-permute-start.1
  34.1 0.1 bitcast_convert_fusion.own
  34.2 0.0 copy-done.1
  34.2 0.0 copy-start
  34.2 0.0 copy-start.2
  34.2 1.9 %shard_map.74 = (f32[512,1024]{1,0:T(8,128)S(1)}, bf16[512,128]{1,0:T(8,128)(2,1)S(1)}, bf16[512,256]{1,0:T(8,128)(2,1)S(1)}) custom-call(f32[1792,128]{1,0:T(8,128)S(1)} %bitcast_convert_fusion.own, bf16[384,1024]{1,0:T(8,128)(2,1)S(1)} %copy-done.1), custom_call_target="tpu_custom_call" | custom-call | tf_op jit(solution)/shard_map/pallas_call | solution.py:369
  36.1 3.8 %collective-permute-done = f16[16,64,128]{2,1,0:T(8,128)(2,1)S(1)} collective-permute-done((f16[16,64,128]{2,1,0:T(8,128)(2,1)S(1)}, f16[16,64,128]{2,1,0:T(8,128)(2,1)S(1)}, u32[]{:S(2)}, u32[]{:S(2)}) %collective-permute-start) | collective-permute-done | bytes 262176 | tf_op jit(solution)/shard_map/ppermute | solution.py:479
  39.9 1.9 %collective-permute-done.1 = f16[16,64,128]{2,1,0:T(8,128)(2,1)S(1)} collective-permute-done((f16[16,64,128]{2,1,0:T(8,128)(2,1)S(1)}, f16[16,64,128]{2,1,0:T(8,128)(2,1)S(1)}, u32[]{:S(2)}, u32[]{:S(2)}) %collective-permute-start.1) | collective-permute-done | bytes 262176 | tf_op jit(solution)/shard_map/ppermute | solution.py:478
  41.8 0.2 fusion
  41.9 0.1 bitcast_convert_fusion.1
  42.1 0.0 copy-done
  42.1 0.0 copy-done.2
  42.1 10.7 %shard_map.75 = (f32[512,384]{1,0:T(8,128)S(1)}, f32[512,384]{1,0:T(8,128)S(1)}) custom-call(f32[1792,128]{1,0:T(8,128)S(1)} %bitcast_convert_fusion.own, f32[1024,128]{1,0:T(8,128)S(1)} %get-tuple-element.24.left, f32[1024,128]{1,0:T(8,128)S(1)} %get-tuple-element.23.right, bf16[512,1024]{1,0:T(8,128)(2,1)S(1)} %copy-done, bf16[512,384]{1,0:T(8,128)(2,1)S(1)} %copy-done.2, ...), custom_call_target="tpu_custom_call" | custom-call | tf_op jit(solution)/shard_map/pallas_call | solution.py:388
  52.8 0.1 convert_element_type.13
  52.9 17.8 %all_to_all.11 = f16[16,32,384]{2,1,0:T(8,128)(2,1)S(1)} all-to-all(f16[16,32,384]{2,1,0:T(8,128)(2,1)S(1)} %bitcast.13), channel_id=1, replica_groups=mesh['lat'=16,'lon'=16] {'lat'}, dimensions={0} | all-to-all | bytes 786432 | tf_op jit(solution)/shard_map/all_to_all | solution.py:485
  70.7 1.0 %convert_multiply_fusion = f32[16,32,384]{2,1,0:T(8,128)} fusion(f32[16,32,384]{2,1,0:T(8,128)S(1)} %bitcast.12, f16[16,32,384]{2,1,0:T(8,128)(2,1)S(1)} %all_to_all.11), kind=kLoop, calls=%fused_computation | loop fusion | flops 393216 | bytes 1966080 | tf_op jit(solution)/shard_map/mul | solution.py:486
Async XLA Ops:
  28.8 5.4 %copy-start.1 = (bf16[384,1024]{1,0:T(8,128)(2,1)S(1)}, bf16[384,1024]{1,0:T(8,128)(2,1)}, u32[]{:S(2)}) copy-start(bf16[384,1024]{1,0:T(8,128)(2,1)} %constant.8.clone.spread) | copy-start | bytes 2359300
  29.0 10.8 %collective-permute-start = (f16[16,64,128]{2,1,0:T(8,128)(2,1)S(1)}, f16[16,64,128]{2,1,0:T(8,128)(2,1)S(1)}, u32[]{:S(2)}, u32[]{:S(2)}) collective-permute-start(f16[16,64,128]{2,1,0:T(8,128)(2,1)S(1)} %slice_select_fusion.1), channel_id=1, source_target_pairs={{0,15},{1,2},{2,1},{3,4},{4,3},{5,6},{6,5},{7,8},{8,7},{9,10},{10,... | collective-permute-start | bytes 786440 | tf_op jit(solution)/shard_map/ppermute | solution.py:479
  34.1 7.7 %collective-permute-start.1 = (f16[16,64,128]{2,1,0:T(8,128)(2,1)S(1)}, f16[16,64,128]{2,1,0:T(8,128)(2,1)S(1)}, u32[]{:S(2)}, u32[]{:S(2)}) collective-permute-start(f16[16,64,128]{2,1,0:T(8,128)(2,1)S(1)} %get-tuple-element.19), channel_id=1, source_target_pairs={{0,1},{1,0},{2,3},{3,2},{4,5},{5,4},{6,7},{7,6},{8,9},{9,8},{10,11... | collective-permute-start | bytes 786440 | tf_op jit(solution)/shard_map/ppermute | solution.py:478
  34.2 7.9 %copy-start = (bf16[512,1024]{1,0:T(8,128)(2,1)S(1)}, bf16[512,1024]{1,0:T(8,128)(2,1)}, u32[]{:S(2)}) copy-start(bf16[512,1024]{1,0:T(8,128)(2,1)} %constant.9.clone.spread) | copy-start | bytes 3145732
  34.2 7.9 %copy-start.2 = (bf16[512,384]{1,0:T(8,128)(2,1)S(1)}, bf16[512,384]{1,0:T(8,128)(2,1)}, u32[]{:S(2)}) copy-start(bf16[512,384]{1,0:T(8,128)(2,1)} %constant.10.clone.collect) | copy-start | bytes 1179652

commit v3 on v2

--- a/solution.py
+++ b/solution.py
@@ -479,8 +479,10 @@
     got1 = lax.ppermute(jnp.where(even, to_left, to_right), "lon", pairs1)
     own = held.astype(f32).reshape(16 * OWN_ROWS, 128)
     parts = core_own(own)
-    left = jnp.where(even, got1, got0).astype(f32).reshape(16 * HALO_ROWS, 128)
-    right = jnp.where(even, got0, got1).astype(f32).reshape(16 * HALO_ROWS, 128)
+    got0 = lax.optimization_barrier(got0.astype(f32))
+    got1 = got1.astype(f32)
+    left = jnp.where(even, got1, got0).reshape(16 * HALO_ROWS, 128)
+    right = jnp.where(even, got0, got1).reshape(16 * HALO_ROWS, 128)
     done, bound = core(own, left, right, parts)
     back = lax.all_to_all(done.astype(jnp.float16).reshape(16, 32, 384), "lat", 0, 0, tiled=True)
     return (back.astype(f32) * bound.reshape(back.shape)).reshape(increments.shape)

time: 71.8 us -> 71.3 us (level)
  waiting for transfers between devices: 5.71 us -> 4.75 us
    ppermute x1, waiting for transfers between devices: 1.89 us -> 0.27 us  [local(): got0 = lax.ppermute(jnp.where(even, to_right, to_left), 'lon', pairs0)]
    ppermute x1, starting transfers between devices: 0.01 us -> 1.3 us  [local(): got0 = lax.ppermute(jnp.where(even, to_right, to_left), 'lon', pairs0)]
    ppermute x1, starting transfers between devices: 5.02 us -> 4.27 us  [local(): got1 = lax.ppermute(jnp.where(even, to_left, to_right), 'lon', pairs1)]
where the time goes in v3:
time: 71.3 us; the launch traced here: 71.1 us
  blocking collectives  43.6 us (61%)
  Pallas kernels  14.2 us (20%)
  starting transfers between devices  5.56 us (8%)
  waiting for transfers between devices  4.75 us (7%)
  other arithmetic  1.62 us (2%)
  between operations  1.4 us (2%)
    all_to_all x1, blocking collectives, local(): held = lax.all_to_all(mine.astype(jnp.float16), 'lat', 0, 0, tiled=True)  25.7 us
    all_to_all x1, blocking collectives, local(): lax.all_to_all(done.astype(jnp.float16).reshape(16, 32, 384), 'lat', 0, 0...  17.8 us
    pallas_call x1, Pallas kernels, core(): pl.pallas_call(kernel, out_shape=(jax.ShapeDtypeStruct((512, 384), f32),...  10.7 us
    ppermute x1, waiting for transfers between devices, local(): got1 = lax.ppermute(jnp.where(even, to_left, to_right), 'lon', pairs1)  4.48 us
    ppermute x1, starting transfers between devices, local(): got1 = lax.ppermute(jnp.where(even, to_left, to_right), 'lon', pairs1)  4.27 us
    pallas_call x1, Pallas kernels, core_own(): pl.pallas_call(own_kernel, out_shape=(jax.ShapeDtypeStruct((512, 1024), f...  1.84 us
    pallas_call x1, Pallas kernels, parcel(): pl.pallas_call(parcel_kernel, out_shape=(jax.ShapeDtypeStruct((16, OWN_RO...  1.63 us
  transfers between devices with their start and end apart: 2, of which 2 were waited for; matrix products, arithmetic and copies ran while one was open for 0% of the time, Pallas kernels for 3%

profile of v3, /device:TPU:1, one launch (start us, length us, event | category | flops | bytes accessed | tf_op | source)
XLA Modules:
  0.0 71.1 jit_solution(626176678997947295)
XLA Ops:
  1.3 1.6 %shard_map.73 = (f32[16,112,128]{2,1,0:T(8,128)S(1)}, f32[16,64,128]{2,1,0:T(8,128)S(1)}) custom-call(s32[1]{0:T(128)S(6)} %copy.8.lat_first, s32[1]{0:T(128)S(6)} %copy.9.lon_first, f32[2,8,32,384]{3,2,1,0:T(8,128)} %increments_hbm.1, bf16[2,8,8,96]{3,2,1,0:T(8,128)(2,1)} %winds_hbm.1), custom_call_target="tpu_custom_call" | custom-call | tf_op jit(solution)/shard_map/pallas_call | solution.py:453
  2.9 0.1 convert_element_type.16
  3.0 25.7 %all_to_all.10 = f16[16,112,128]{2,1,0:T(8,128)(2,1)S(1)} all-to-all(f16[16,112,128]{2,1,0:T(8,128)(2,1)S(1)} %convert_element_type.16), channel_id=1, replica_groups=mesh['lat'=16,'lon'=16] {'lat'}, dimensions={0} | all-to-all | bytes 917504 | tf_op jit(solution)/shard_map/all_to_all | solution.py:473
  28.8 0.0 copy-start.1
  28.8 0.2 slice_select_fusion.1
  28.9 0.1 slice_select_fusion
  29.0 1.3 %collective-permute-start.1 = (f16[16,64,128]{2,1,0:T(8,128)(2,1)S(1)}, f16[16,64,128]{2,1,0:T(8,128)(2,1)S(1)}, u32[]{:S(2)}, u32[]{:S(2)}) collective-permute-start(f16[16,64,128]{2,1,0:T(8,128)(2,1)S(1)} %slice_select_fusion), channel_id=1, source_target_pairs={{0,1},{1,0},{2,3},{3,2},{4,5},{5,4},{6,7},{7,6},{8,9},{9,8},{10,11... | collective-permute-start | bytes 786440 | tf_op jit(solution)/shard_map/ppermute | solution.py:478
  30.3 4.3 %collective-permute-start = (f16[16,64,128]{2,1,0:T(8,128)(2,1)S(1)}, f16[16,64,128]{2,1,0:T(8,128)(2,1)S(1)}, u32[]{:S(2)}, u32[]{:S(2)}) collective-permute-start(f16[16,64,128]{2,1,0:T(8,128)(2,1)S(1)} %get-tuple-element.19), channel_id=1, source_target_pairs={{0,15},{1,2},{2,1},{3,4},{4,3},{5,6},{6,5},{7,8},{8,7},{9,10},{10,... | collective-permute-start | bytes 786440 | tf_op jit(solution)/shard_map/ppermute | solution.py:479
  34.6 0.1 bitcast_convert_fusion.own
  34.7 0.0 copy-done.1
  34.7 0.0 copy-start
  34.7 0.0 copy-start.2
  34.7 1.8 %shard_map.74 = (f32[512,1024]{1,0:T(8,128)S(1)}, bf16[512,128]{1,0:T(8,128)(2,1)S(1)}, bf16[512,256]{1,0:T(8,128)(2,1)S(1)}) custom-call(f32[1792,128]{1,0:T(8,128)S(1)} %bitcast_convert_fusion.own, bf16[384,1024]{1,0:T(8,128)(2,1)S(1)} %copy-done.1), custom_call_target="tpu_custom_call" | custom-call | tf_op jit(solution)/shard_map/pallas_call | solution.py:369
  36.6 0.3 collective-permute-done.1
  36.9 4.5 %collective-permute-done = f16[16,64,128]{2,1,0:T(8,128)(2,1)S(1)} collective-permute-done((f16[16,64,128]{2,1,0:T(8,128)(2,1)S(1)}, f16[16,64,128]{2,1,0:T(8,128)(2,1)S(1)}, u32[]{:S(2)}, u32[]{:S(2)}) %collective-permute-start) | collective-permute-done | bytes 262176 | tf_op jit(solution)/shard_map/ppermute | solution.py:479
  41.4 0.1 convert_select_fusion
  41.5 0.0 copy-done
  41.5 0.0 copy-done.2
  41.5 10.7 %shard_map.75 = (f32[512,384]{1,0:T(8,128)S(1)}, f32[512,384]{1,0:T(8,128)S(1)}) custom-call(f32[1792,128]{1,0:T(8,128)S(1)} %bitcast_convert_fusion.own, f32[1024,128]{1,0:T(8,128)S(1)} %bitcast.9, f32[1024,128]{1,0:T(8,128)S(1)} %bitcast.8, bf16[512,1024]{1,0:T(8,128)(2,1)S(1)} %copy-done, bf16[512,384]{1,0:T(8,128)(2,1)S(1)} %copy-done.2, ...), custom_call_target="tpu_custom_call" | custom-call | tf_op jit(solution)/shard_map/pallas_call | solution.py:388
  52.3 0.1 convert_element_type.19
  52.3 17.8 %all_to_all.11 = f16[16,32,384]{2,1,0:T(8,128)(2,1)S(1)} all-to-all(f16[16,32,384]{2,1,0:T(8,128)(2,1)S(1)} %bitcast.11), channel_id=1, replica_groups=mesh['lat'=16,'lon'=16] {'lat'}, dimensions={0} | all-to-all | bytes 786432 | tf_op jit(solution)/shard_map/all_to_all | solution.py:487
  70.1 1.0 %convert_multiply_fusion = f32[16,32,384]{2,1,0:T(8,128)} fusion(f32[16,32,384]{2,1,0:T(8,128)S(1)} %bitcast.10, f16[16,32,384]{2,1,0:T(8,128)(2,1)S(1)} %all_to_all.11), kind=kLoop, calls=%fused_computation | loop fusion | flops 393216 | bytes 1966080 | tf_op jit(solution)/shard_map/mul | solution.py:488
  (1 shorter events, 0.0 us)
Async XLA Ops:
  28.8 6.0 %copy-start.1 = (bf16[384,1024]{1,0:T(8,128)(2,1)S(1)}, bf16[384,1024]{1,0:T(8,128)(2,1)}, u32[]{:S(2)}) copy-start(bf16[384,1024]{1,0:T(8,128)(2,1)} %constant.8.clone.spread) | copy-start | bytes 2359300
  29.0 7.8 %collective-permute-start.1 = (f16[16,64,128]{2,1,0:T(8,128)(2,1)S(1)}, f16[16,64,128]{2,1,0:T(8,128)(2,1)S(1)}, u32[]{:S(2)}, u32[]{:S(2)}) collective-permute-start(f16[16,64,128]{2,1,0:T(8,128)(2,1)S(1)} %slice_select_fusion), channel_id=1, source_target_pairs={{0,1},{1,0},{2,3},{3,2},{4,5},{5,4},{6,7},{7,6},{8,9},{9,8},{10,11... | collective-permute-start | bytes 786440 | tf_op jit(solution)/shard_map/ppermute | solution.py:478
  30.3 11.0 %collective-permute-start = (f16[16,64,128]{2,1,0:T(8,128)(2,1)S(1)}, f16[16,64,128]{2,1,0:T(8,128)(2,1)S(1)}, u32[]{:S(2)}, u32[]{:S(2)}) collective-permute-start(f16[16,64,128]{2,1,0:T(8,128)(2,1)S(1)} %get-tuple-element.19), channel_id=1, source_target_pairs={{0,15},{1,2},{2,1},{3,4},{4,3},{5,6},{6,5},{7,8},{8,7},{9,10},{10,... | collective-permute-start | bytes 786440 | tf_op jit(solution)/shard_map/ppermute | solution.py:479
  34.7 6.8 %copy-start = (bf16[512,1024]{1,0:T(8,128)(2,1)S(1)}, bf16[512,1024]{1,0:T(8,128)(2,1)}, u32[]{:S(2)}) copy-start(bf16[512,1024]{1,0:T(8,128)(2,1)} %constant.9.clone.spread) | copy-start | bytes 3145732
  34.7 6.8 %copy-start.2 = (bf16[512,384]{1,0:T(8,128)(2,1)S(1)}, bf16[512,384]{1,0:T(8,128)(2,1)}, u32[]{:S(2)}) copy-start(bf16[512,384]{1,0:T(8,128)(2,1)} %constant.10.clone.collect) | copy-start | bytes 1179652

commit v4 on v3

--- a/solution.py
+++ b/solution.py
@@ -56,6 +56,52 @@
 def east(v, hop):
     last = pltpu.roll(v[0], 128 - hop, 1)[None]
     return jnp.concatenate([v[1:], last], 0) if v.shape[0] > 1 else last
+
+
+def packed_west(v):
+    middle = middle_lanes()
+    first = jnp.where(middle, pltpu.roll(v[-1], 65, 1), pltpu.roll(v[-1], 64, 1))
+    return jnp.concatenate([first[None], v[:-1]], 0)
+
+
+def packed_east(v):
+    middle = middle_lanes()
+    last = jnp.where(middle, pltpu.roll(v[0], 64, 1), pltpu.roll(v[0], 63, 1))
+    return jnp.concatenate([v[1:], last[None]], 0)
+
+
+def middle_lanes():
+    lane = lax.broadcasted_iota(jnp.int32, (8, 128), 1)
+    return (lane >= 32) & (lane < 96)
+
+
+def packed(v):
+    half = PHASES // 2
+    return jnp.concatenate([jnp.where(middle_lanes(), v[p], pltpu.roll(v[p + half], 64, 1))[None] for p in range(half)], 0)
+
+
+def last_sweeps(x, b, coarse, y):
+    gain = OMEGA / centre(0)
+    old = lambda r: packed(x[r] + doubled(coarse[r // 2], PHASES))
+
+    def run(old, b_of, last):
+        first = old(0)
+        prev, here = above_first(old(ROWS - 1)), first
+        for r in range(ROWS):
+            below = old(r + 1) if r < ROWS - 1 else below_last(first)
+            near = (prev + below) + (packed_west(here) + packed_east(here))
+            last(r, 0.2 * here + gain * (b_of(r) + near))
+            prev, here = here, below
+
+    def keep(r, value):
+        y[r] = value
+
+    def keep_b(r):
+        y[ROWS + r] = packed(b[r])
+        return y[ROWS + r]
+
+    run(old, keep_b, keep)
+    run(lambda r: y[r], lambda r: y[ROWS + r], keep)
 
 
 def above_first(v):
@@ -175,7 +221,7 @@
     x[rows] = jnp.zeros(x.shape[1:], f32)
 
 
-def vcycle(level, x, b, fresh):
+def vcycle(level, x, b, fresh, last=None):
     if level == GRIDS - 1:
         coarsest(x[level], b[level])
         return
@@ -186,6 +232,9 @@
         sweep(level, x[level], b[level])
     residual(level, x[level], b[level], b[level + 1])
     vcycle(level + 1, x, b, True)
+    if last is not None:
+        last_sweeps(x[level], b[level], x[level + 1], last)
+        return
     sweep(level, x[level], b[level], coarse=x[level + 1])
     sweep(level, x[level], b[level])
     if level > 0:
@@ -283,7 +332,7 @@
     winds[...] = row_winds(table, (own, OWN_ROWS, 64, OWN_NUMBER), (own, OWN_ROWS, 32, OWN_NUMBER))
 
 
-def kernel(own, left, right, spread, collect, force0, row_table, winds, out, bound, x0, x1, x2, x3, x4, b0, b1, b2, b3, b4, gx, gy, split, flat):
+def kernel(own, left, right, spread, collect, force0, row_table, winds, out, bound, x0, x1, x2, x3, x4, b0, b1, b2, b3, b4, gx, gy, split, flat, y):
     x = (x0, x1, x2, x3, x4)
     b = (b0, b1, b2, b3, b4)
     spread_rows(
@@ -337,18 +386,15 @@
     b0[ROWS] = below_last(b0[0])
 
     for cycle in range(CYCLES):
-        vcycle(0, x, b, cycle == 0)
+        vcycle(0, x, b, cycle == 0, y if cycle == CYCLES - 1 else None)
 
     powers = own_number(own, OWN_ROWS, *OWN_NUMBER) + own_number(left, HALO_ROWS, *LEFT_NUMBER) + own_number(right, HALO_ROWS, *RIGHT_NUMBER)
     power = jnp.max(functools.reduce(jnp.maximum, powers), axis=0, keepdims=True) + (GAIN_EXP - IN_EXP)
     bound[...] = jnp.broadcast_to(jnp.exp2(power), (512, 384))
     scale = jnp.exp2(-power)
-    lane = lax.broadcasted_iota(jnp.int32, (8, 128), 1)
-    inside = (lane >= LEAD) & (lane < LEAD + 48)
     for s in range(ROWS // 2):
         for p in range(PHASES // 2):
-            pair = [jnp.where(inside, x0[r, p], pltpu.roll(x0[r, p + 4], 64, 1)) for r in (2 * s, 2 * s + 1)]
-            pair = jnp.concatenate(pair, 0) * scale
+            pair = jnp.concatenate([y[2 * s, p], y[2 * s + 1, p]], 0) * scale
             high = pair.astype(bf16)
             split[16 * s : 16 * s + 16, 128 * p : 128 * p + 128] = high
             split[16 * s : 16 * s + 16, 512 + 128 * p : 640 + 128 * p] = (pair - high.astype(f32)).astype(bf16)
@@ -395,6 +441,7 @@
             pltpu.VMEM((512, 1024), f32),
             pltpu.VMEM((512, 1024), bf16),
             pltpu.VMEM((1536, 128), f32),
+            pltpu.VMEM((2 * ROWS, PHASES // 2, 8, 128), f32),
         ],
         interpret=interpret,
         **PARAMS,

time: 71.3 us -> 71 us (level)
  no operation moved by 1% of the time
where the time goes in v4:
time: 71 us; the launch traced here: 70.8 us
  blocking collectives  43.6 us (61%)
  Pallas kernels  13.9 us (20%)
  starting transfers between devices  5.56 us (8%)
  waiting for transfers between devices  4.75 us (7%)
  other arithmetic  1.62 us (2%)
  between operations  1.4 us (2%)
    all_to_all x1, blocking collectives, local(): held = lax.all_to_all(mine.astype(jnp.float16), 'lat', 0, 0, tiled=True)  25.7 us
    all_to_all x1, blocking collectives, local(): lax.all_to_all(done.astype(jnp.float16).reshape(16, 32, 384), 'lat', 0, 0...  17.8 us
    pallas_call x1, Pallas kernels, core(): pl.pallas_call(kernel, out_shape=(jax.ShapeDtypeStruct((512, 384), f32),...  10.4 us
    ppermute x1, waiting for transfers between devices, local(): got1 = lax.ppermute(jnp.where(even, to_left, to_right), 'lon', pairs1)  4.48 us
    ppermute x1, starting transfers between devices, local(): got1 = lax.ppermute(jnp.where(even, to_left, to_right), 'lon', pairs1)  4.27 us
    pallas_call x1, Pallas kernels, core_own(): pl.pallas_call(own_kernel, out_shape=(jax.ShapeDtypeStruct((512, 1024), f...  1.84 us
    pallas_call x1, Pallas kernels, parcel(): pl.pallas_call(parcel_kernel, out_shape=(jax.ShapeDtypeStruct((16, OWN_RO...  1.63 us
  transfers between devices with their start and end apart: 2, of which 2 were waited for; matrix products, arithmetic and copies ran while one was open for 0% of the time, Pallas kernels for 3%

profile of v4, /device:TPU:1, one launch (start us, length us, event | category | flops | bytes accessed | tf_op | source)
XLA Modules:
  0.0 70.8 jit_solution(13359883021478452896)
XLA Ops:
  1.3 1.6 %shard_map.73 = (f32[16,112,128]{2,1,0:T(8,128)S(1)}, f32[16,64,128]{2,1,0:T(8,128)S(1)}) custom-call(s32[1]{0:T(128)S(6)} %copy.8.lat_first, s32[1]{0:T(128)S(6)} %copy.9.lon_first, f32[2,8,32,384]{3,2,1,0:T(8,128)} %increments_hbm.1, bf16[2,8,8,96]{3,2,1,0:T(8,128)(2,1)} %winds_hbm.1), custom_call_target="tpu_custom_call" | custom-call | tf_op jit(solution)/shard_map/pallas_call | solution.py:500
  2.9 0.1 convert_element_type.16
  3.0 25.7 %all_to_all.10 = f16[16,112,128]{2,1,0:T(8,128)(2,1)S(1)} all-to-all(f16[16,112,128]{2,1,0:T(8,128)(2,1)S(1)} %convert_element_type.16), channel_id=1, replica_groups=mesh['lat'=16,'lon'=16] {'lat'}, dimensions={0} | all-to-all | bytes 917504 | tf_op jit(solution)/shard_map/all_to_all | solution.py:520
  28.8 0.0 copy-start.1
  28.8 0.2 slice_select_fusion.1
  28.9 0.1 slice_select_fusion
  29.0 1.3 %collective-permute-start.1 = (f16[16,64,128]{2,1,0:T(8,128)(2,1)S(1)}, f16[16,64,128]{2,1,0:T(8,128)(2,1)S(1)}, u32[]{:S(2)}, u32[]{:S(2)}) collective-permute-start(f16[16,64,128]{2,1,0:T(8,128)(2,1)S(1)} %slice_select_fusion), channel_id=1, source_target_pairs={{0,1},{1,0},{2,3},{3,2},{4,5},{5,4},{6,7},{7,6},{8,9},{9,8},{10,11... | collective-permute-start | bytes 786440 | tf_op jit(solution)/shard_map/ppermute | solution.py:525
  30.3 4.3 %collective-permute-start = (f16[16,64,128]{2,1,0:T(8,128)(2,1)S(1)}, f16[16,64,128]{2,1,0:T(8,128)(2,1)S(1)}, u32[]{:S(2)}, u32[]{:S(2)}) collective-permute-start(f16[16,64,128]{2,1,0:T(8,128)(2,1)S(1)} %get-tuple-element.19), channel_id=1, source_target_pairs={{0,15},{1,2},{2,1},{3,4},{4,3},{5,6},{6,5},{7,8},{8,7},{9,10},{10,... | collective-permute-start | bytes 786440 | tf_op jit(solution)/shard_map/ppermute | solution.py:526
  34.6 0.1 bitcast_convert_fusion.own
  34.7 0.0 copy-done.1
  34.7 0.0 copy-start
  34.7 0.0 copy-start.2
  34.7 1.8 %shard_map.74 = (f32[512,1024]{1,0:T(8,128)S(1)}, bf16[512,128]{1,0:T(8,128)(2,1)S(1)}, bf16[512,256]{1,0:T(8,128)(2,1)S(1)}) custom-call(f32[1792,128]{1,0:T(8,128)S(1)} %bitcast_convert_fusion.own, bf16[384,1024]{1,0:T(8,128)(2,1)S(1)} %copy-done.1), custom_call_target="tpu_custom_call" | custom-call | tf_op jit(solution)/shard_map/pallas_call | solution.py:415
  36.6 0.3 collective-permute-done.1
  36.9 4.5 %collective-permute-done = f16[16,64,128]{2,1,0:T(8,128)(2,1)S(1)} collective-permute-done((f16[16,64,128]{2,1,0:T(8,128)(2,1)S(1)}, f16[16,64,128]{2,1,0:T(8,128)(2,1)S(1)}, u32[]{:S(2)}, u32[]{:S(2)}) %collective-permute-start) | collective-permute-done | bytes 262176 | tf_op jit(solution)/shard_map/ppermute | solution.py:526
  41.4 0.1 convert_select_fusion
  41.5 0.0 copy-done
  41.5 0.0 copy-done.2
  41.5 10.4 %shard_map.75 = (f32[512,384]{1,0:T(8,128)S(1)}, f32[512,384]{1,0:T(8,128)S(1)}) custom-call(f32[1792,128]{1,0:T(8,128)S(1)} %bitcast_convert_fusion.own, f32[1024,128]{1,0:T(8,128)S(1)} %bitcast.9, f32[1024,128]{1,0:T(8,128)S(1)} %bitcast.8, bf16[512,1024]{1,0:T(8,128)(2,1)S(1)} %copy-done, bf16[512,384]{1,0:T(8,128)(2,1)S(1)} %copy-done.2, ...), custom_call_target="tpu_custom_call" | custom-call | tf_op jit(solution)/shard_map/pallas_call | solution.py:434
  51.9 0.1 convert_element_type.19
  52.0 17.8 %all_to_all.11 = f16[16,32,384]{2,1,0:T(8,128)(2,1)S(1)} all-to-all(f16[16,32,384]{2,1,0:T(8,128)(2,1)S(1)} %bitcast.11), channel_id=1, replica_groups=mesh['lat'=16,'lon'=16] {'lat'}, dimensions={0} | all-to-all | bytes 786432 | tf_op jit(solution)/shard_map/all_to_all | solution.py:534
  69.8 1.0 %convert_multiply_fusion = f32[16,32,384]{2,1,0:T(8,128)} fusion(f32[16,32,384]{2,1,0:T(8,128)S(1)} %bitcast.10, f16[16,32,384]{2,1,0:T(8,128)(2,1)S(1)} %all_to_all.11), kind=kLoop, calls=%fused_computation | loop fusion | flops 393216 | bytes 1966080 | tf_op jit(solution)/shard_map/mul | solution.py:535
  (1 shorter events, 0.0 us)
Async XLA Ops:
  28.8 6.0 %copy-start.1 = (bf16[384,1024]{1,0:T(8,128)(2,1)S(1)}, bf16[384,1024]{1,0:T(8,128)(2,1)}, u32[]{:S(2)}) copy-start(bf16[384,1024]{1,0:T(8,128)(2,1)} %constant.8.clone.spread) | copy-start | bytes 2359300
  29.0 7.8 %collective-permute-start.1 = (f16[16,64,128]{2,1,0:T(8,128)(2,1)S(1)}, f16[16,64,128]{2,1,0:T(8,128)(2,1)S(1)}, u32[]{:S(2)}, u32[]{:S(2)}) collective-permute-start(f16[16,64,128]{2,1,0:T(8,128)(2,1)S(1)} %slice_select_fusion), channel_id=1, source_target_pairs={{0,1},{1,0},{2,3},{3,2},{4,5},{5,4},{6,7},{7,6},{8,9},{9,8},{10,11... | collective-permute-start | bytes 786440 | tf_op jit(solution)/shard_map/ppermute | solution.py:525
  30.3 11.0 %collective-permute-start = (f16[16,64,128]{2,1,0:T(8,128)(2,1)S(1)}, f16[16,64,128]{2,1,0:T(8,128)(2,1)S(1)}, u32[]{:S(2)}, u32[]{:S(2)}) collective-permute-start(f16[16,64,128]{2,1,0:T(8,128)(2,1)S(1)} %get-tuple-element.19), channel_id=1, source_target_pairs={{0,15},{1,2},{2,1},{3,4},{4,3},{5,6},{6,5},{7,8},{8,7},{9,10},{10,... | collective-permute-start | bytes 786440 | tf_op jit(solution)/shard_map/ppermute | solution.py:526
  34.7 6.8 %copy-start = (bf16[512,1024]{1,0:T(8,128)(2,1)S(1)}, bf16[512,1024]{1,0:T(8,128)(2,1)}, u32[]{:S(2)}) copy-start(bf16[512,1024]{1,0:T(8,128)(2,1)} %constant.9.clone.spread) | copy-start | bytes 3145732
  34.7 6.8 %copy-start.2 = (bf16[512,384]{1,0:T(8,128)(2,1)S(1)}, bf16[512,384]{1,0:T(8,128)(2,1)}, u32[]{:S(2)}) copy-start(bf16[512,384]{1,0:T(8,128)(2,1)} %constant.10.clone.collect) | copy-start | bytes 1179652

commit v5 on v4

--- a/solution.py
+++ b/solution.py
@@ -76,19 +76,23 @@
 
 
 def packed(v):
-    half = PHASES // 2
+    half = v.shape[0] // 2
     return jnp.concatenate([jnp.where(middle_lanes(), v[p], pltpu.roll(v[p + half], 64, 1))[None] for p in range(half)], 0)
 
 
-def last_sweeps(x, b, coarse, y):
-    gain = OMEGA / centre(0)
-    old = lambda r: packed(x[r] + doubled(coarse[r // 2], PHASES))
+def last_sweeps(level, x, b, coarse, y):
+    rows, phases, _ = shape_of(level)
+    gain = OMEGA / centre(level)
+    if level == 0:
+        old = lambda r: packed(x[r]) + doubled(coarse[r // 2], phases // 2)
+    else:
+        old = lambda r: packed(x[r] + doubled(coarse[r // 2], phases))
 
     def run(old, b_of, last):
         first = old(0)
-        prev, here = above_first(old(ROWS - 1)), first
-        for r in range(ROWS):
-            below = old(r + 1) if r < ROWS - 1 else below_last(first)
+        prev, here = above_first(old(rows - 1)), first
+        for r in range(rows):
+            below = old(r + 1) if r < rows - 1 else below_last(first)
             near = (prev + below) + (packed_west(here) + packed_east(here))
             last(r, 0.2 * here + gain * (b_of(r) + near))
             prev, here = here, below
@@ -97,11 +101,11 @@
         y[r] = value
 
     def keep_b(r):
-        y[ROWS + r] = packed(b[r])
-        return y[ROWS + r]
+        y[rows + r] = packed(b[r])
+        return y[rows + r]
 
     run(old, keep_b, keep)
-    run(lambda r: y[r], lambda r: y[ROWS + r], keep)
+    run(lambda r: y[r], lambda r: y[rows + r], keep)
 
 
 def above_first(v):
@@ -231,9 +235,9 @@
         sweep(level, x[level], b[level])
         sweep(level, x[level], b[level])
     residual(level, x[level], b[level], b[level + 1])
-    vcycle(level + 1, x, b, True)
-    if last is not None:
-        last_sweeps(x[level], b[level], x[level + 1], last)
+    vcycle(level + 1, x, b, True, last[1:] if last else None)
+    if last:
+        last_sweeps(level, x[level], b[level], last[1] if level == 0 else x[level + 1], last[0])
         return
     sweep(level, x[level], b[level], coarse=x[level + 1])
     sweep(level, x[level], b[level])
@@ -332,7 +336,7 @@
     winds[...] = row_winds(table, (own, OWN_ROWS, 64, OWN_NUMBER), (own, OWN_ROWS, 32, OWN_NUMBER))
 
 
-def kernel(own, left, right, spread, collect, force0, row_table, winds, out, bound, x0, x1, x2, x3, x4, b0, b1, b2, b3, b4, gx, gy, split, flat, y):
+def kernel(own, left, right, spread, collect, force0, row_table, winds, out, bound, x0, x1, x2, x3, x4, b0, b1, b2, b3, b4, gx, gy, split, flat, y, y1):
     x = (x0, x1, x2, x3, x4)
     b = (b0, b1, b2, b3, b4)
     spread_rows(
@@ -386,7 +390,7 @@
     b0[ROWS] = below_last(b0[0])
 
     for cycle in range(CYCLES):
-        vcycle(0, x, b, cycle == 0, y if cycle == CYCLES - 1 else None)
+        vcycle(0, x, b, cycle == 0, (y, y1) if cycle == CYCLES - 1 else None)
 
     powers = own_number(own, OWN_ROWS, *OWN_NUMBER) + own_number(left, HALO_ROWS, *LEFT_NUMBER) + own_number(right, HALO_ROWS, *RIGHT_NUMBER)
     power = jnp.max(functools.reduce(jnp.maximum, powers), axis=0, keepdims=True) + (GAIN_EXP - IN_EXP)
@@ -442,6 +446,7 @@
             pltpu.VMEM((512, 1024), bf16),
             pltpu.VMEM((1536, 128), f32),
             pltpu.VMEM((2 * ROWS, PHASES // 2, 8, 128), f32),
+            pltpu.VMEM((ROWS, PHASES // 4, 8, 128), f32),
         ],
         interpret=interpret,
         **PARAMS,

time: 71 us -> 71.2 us (level)
  no operation moved by 1% of the time
where the time goes in v5:
time: 71.2 us; the launch traced here: 71 us
  blocking collectives  43.6 us (61%)
  Pallas kernels  14.1 us (20%)
  starting transfers between devices  5.56 us (8%)
  waiting for transfers between devices  4.75 us (7%)
  other arithmetic  1.62 us (2%)
  between operations  1.4 us (2%)
    all_to_all x1, blocking collectives, local(): held = lax.all_to_all(mine.astype(jnp.float16), 'lat', 0, 0, tiled=True)  25.7 us
    all_to_all x1, blocking collectives, local(): lax.all_to_all(done.astype(jnp.float16).reshape(16, 32, 384), 'lat', 0, 0...  17.8 us
    pallas_call x1, Pallas kernels, core(): pl.pallas_call(kernel, out_shape=(jax.ShapeDtypeStruct((512, 384), f32),...  10.6 us
    ppermute x1, waiting for transfers between devices, local(): got1 = lax.ppermute(jnp.where(even, to_left, to_right), 'lon', pairs1)  4.48 us
    ppermute x1, starting transfers between devices, local(): got1 = lax.ppermute(jnp.where(even, to_left, to_right), 'lon', pairs1)  4.27 us
    pallas_call x1, Pallas kernels, core_own(): pl.pallas_call(own_kernel, out_shape=(jax.ShapeDtypeStruct((512, 1024), f...  1.84 us
    pallas_call x1, Pallas kernels, parcel(): pl.pallas_call(parcel_kernel, out_shape=(jax.ShapeDtypeStruct((16, OWN_RO...  1.63 us
  transfers between devices with their start and end apart: 2, of which 2 were waited for; matrix products, arithmetic and copies ran while one was open for 0% of the time, Pallas kernels for 3%

profile of v5, /device:TPU:1, one launch (start us, length us, event | category | flops | bytes accessed | tf_op | source)
XLA Modules:
  0.0 71.0 jit_solution(10414560760494897318)
XLA Ops:
  1.3 1.6 %shard_map.73 = (f32[16,112,128]{2,1,0:T(8,128)S(1)}, f32[16,64,128]{2,1,0:T(8,128)S(1)}) custom-call(s32[1]{0:T(128)S(6)} %copy.8.lat_first, s32[1]{0:T(128)S(6)} %copy.9.lon_first, f32[2,8,32,384]{3,2,1,0:T(8,128)} %increments_hbm.1, bf16[2,8,8,96]{3,2,1,0:T(8,128)(2,1)} %winds_hbm.1), custom_call_target="tpu_custom_call" | custom-call | tf_op jit(solution)/shard_map/pallas_call | solution.py:505
  2.9 0.1 convert_element_type.16
  3.0 25.7 %all_to_all.10 = f16[16,112,128]{2,1,0:T(8,128)(2,1)S(1)} all-to-all(f16[16,112,128]{2,1,0:T(8,128)(2,1)S(1)} %convert_element_type.16), channel_id=1, replica_groups=mesh['lat'=16,'lon'=16] {'lat'}, dimensions={0} | all-to-all | bytes 917504 | tf_op jit(solution)/shard_map/all_to_all | solution.py:525
  28.8 0.0 copy-start.1
  28.8 0.2 slice_select_fusion.1
  28.9 0.1 slice_select_fusion
  29.0 1.3 %collective-permute-start.1 = (f16[16,64,128]{2,1,0:T(8,128)(2,1)S(1)}, f16[16,64,128]{2,1,0:T(8,128)(2,1)S(1)}, u32[]{:S(2)}, u32[]{:S(2)}) collective-permute-start(f16[16,64,128]{2,1,0:T(8,128)(2,1)S(1)} %slice_select_fusion), channel_id=1, source_target_pairs={{0,1},{1,0},{2,3},{3,2},{4,5},{5,4},{6,7},{7,6},{8,9},{9,8},{10,11... | collective-permute-start | bytes 786440 | tf_op jit(solution)/shard_map/ppermute | solution.py:530
  30.3 4.3 %collective-permute-start = (f16[16,64,128]{2,1,0:T(8,128)(2,1)S(1)}, f16[16,64,128]{2,1,0:T(8,128)(2,1)S(1)}, u32[]{:S(2)}, u32[]{:S(2)}) collective-permute-start(f16[16,64,128]{2,1,0:T(8,128)(2,1)S(1)} %get-tuple-element.19), channel_id=1, source_target_pairs={{0,15},{1,2},{2,1},{3,4},{4,3},{5,6},{6,5},{7,8},{8,7},{9,10},{10,... | collective-permute-start | bytes 786440 | tf_op jit(solution)/shard_map/ppermute | solution.py:531
  34.6 0.1 bitcast_convert_fusion.own
  34.7 0.0 copy-done.1
  34.7 0.0 copy-start
  34.7 0.0 copy-start.2
  34.7 1.8 %shard_map.74 = (f32[512,1024]{1,0:T(8,128)S(1)}, bf16[512,128]{1,0:T(8,128)(2,1)S(1)}, bf16[512,256]{1,0:T(8,128)(2,1)S(1)}) custom-call(f32[1792,128]{1,0:T(8,128)S(1)} %bitcast_convert_fusion.own, bf16[384,1024]{1,0:T(8,128)(2,1)S(1)} %copy-done.1), custom_call_target="tpu_custom_call" | custom-call | tf_op jit(solution)/shard_map/pallas_call | solution.py:419
  36.6 0.3 collective-permute-done.1
  36.9 4.5 %collective-permute-done = f16[16,64,128]{2,1,0:T(8,128)(2,1)S(1)} collective-permute-done((f16[16,64,128]{2,1,0:T(8,128)(2,1)S(1)}, f16[16,64,128]{2,1,0:T(8,128)(2,1)S(1)}, u32[]{:S(2)}, u32[]{:S(2)}) %collective-permute-start) | collective-permute-done | bytes 262176 | tf_op jit(solution)/shard_map/ppermute | solution.py:531
  41.4 0.1 convert_select_fusion
  41.5 0.0 copy-done
  41.5 0.0 copy-done.2
  41.5 10.6 %shard_map.75 = (f32[512,384]{1,0:T(8,128)S(1)}, f32[512,384]{1,0:T(8,128)S(1)}) custom-call(f32[1792,128]{1,0:T(8,128)S(1)} %bitcast_convert_fusion.own, f32[1024,128]{1,0:T(8,128)S(1)} %bitcast.9, f32[1024,128]{1,0:T(8,128)S(1)} %bitcast.8, bf16[512,1024]{1,0:T(8,128)(2,1)S(1)} %copy-done, bf16[512,384]{1,0:T(8,128)(2,1)S(1)} %copy-done.2, ...), custom_call_target="tpu_custom_call" | custom-call | tf_op jit(solution)/shard_map/pallas_call | solution.py:438
  52.1 0.1 convert_element_type.19
  52.2 17.8 %all_to_all.11 = f16[16,32,384]{2,1,0:T(8,128)(2,1)S(1)} all-to-all(f16[16,32,384]{2,1,0:T(8,128)(2,1)S(1)} %bitcast.11), channel_id=1, replica_groups=mesh['lat'=16,'lon'=16] {'lat'}, dimensions={0} | all-to-all | bytes 786432 | tf_op jit(solution)/shard_map/all_to_all | solution.py:539
  70.0 1.0 %convert_multiply_fusion = f32[16,32,384]{2,1,0:T(8,128)} fusion(f32[16,32,384]{2,1,0:T(8,128)S(1)} %bitcast.10, f16[16,32,384]{2,1,0:T(8,128)(2,1)S(1)} %all_to_all.11), kind=kLoop, calls=%fused_computation | loop fusion | flops 393216 | bytes 1966080 | tf_op jit(solution)/shard_map/mul | solution.py:540
  (1 shorter events, 0.0 us)
Async XLA Ops:
  28.8 6.0 %copy-start.1 = (bf16[384,1024]{1,0:T(8,128)(2,1)S(1)}, bf16[384,1024]{1,0:T(8,128)(2,1)}, u32[]{:S(2)}) copy-start(bf16[384,1024]{1,0:T(8,128)(2,1)} %constant.8.clone.spread) | copy-start | bytes 2359300
  29.0 7.8 %collective-permute-start.1 = (f16[16,64,128]{2,1,0:T(8,128)(2,1)S(1)}, f16[16,64,128]{2,1,0:T(8,128)(2,1)S(1)}, u32[]{:S(2)}, u32[]{:S(2)}) collective-permute-start(f16[16,64,128]{2,1,0:T(8,128)(2,1)S(1)} %slice_select_fusion), channel_id=1, source_target_pairs={{0,1},{1,0},{2,3},{3,2},{4,5},{5,4},{6,7},{7,6},{8,9},{9,8},{10,11... | collective-permute-start | bytes 786440 | tf_op jit(solution)/shard_map/ppermute | solution.py:530
  30.3 11.0 %collective-permute-start = (f16[16,64,128]{2,1,0:T(8,128)(2,1)S(1)}, f16[16,64,128]{2,1,0:T(8,128)(2,1)S(1)}, u32[]{:S(2)}, u32[]{:S(2)}) collective-permute-start(f16[16,64,128]{2,1,0:T(8,128)(2,1)S(1)} %get-tuple-element.19), channel_id=1, source_target_pairs={{0,15},{1,2},{2,1},{3,4},{4,3},{5,6},{6,5},{7,8},{8,7},{9,10},{10,... | collective-permute-start | bytes 786440 | tf_op jit(solution)/shard_map/ppermute | solution.py:531
  34.7 6.8 %copy-start = (bf16[512,1024]{1,0:T(8,128)(2,1)S(1)}, bf16[512,1024]{1,0:T(8,128)(2,1)}, u32[]{:S(2)}) copy-start(bf16[512,1024]{1,0:T(8,128)(2,1)} %constant.9.clone.spread) | copy-start | bytes 3145732
  34.7 6.8 %copy-start.2 = (bf16[512,384]{1,0:T(8,128)(2,1)S(1)}, bf16[512,384]{1,0:T(8,128)(2,1)}, u32[]{:S(2)}) copy-start(bf16[512,384]{1,0:T(8,128)(2,1)} %constant.10.clone.collect) | copy-start | bytes 1179652
